TPU v7x, 256 devices: a whole 4x4x8 slice. The times are simulated.
256 devices in a mesh: cp: 64 (over y, z, core), tp: 4 (over x).
Axes of the slice: x: 4, y: 4, z: 8, core: 2. Of those that a mesh axis runs over, the one named last changes fastest.
Arguments:
- queries: bfloat16 [32768, 4096], P('cp', 'tp'), may hold values from -6 to 6
- key_rows: bfloat16 [32768, 512], P('cp', 'tp'), may hold values from -6 to 6
- value_rows: bfloat16 [32768, 512], P('cp', 'tp'), may hold values from -6 to 6
- out_proj: bfloat16 [4096, 4096], P('tp'), may hold values from -0.09375 to 0.09375
- grad_mixed: bfloat16 [32768, 4096], P('cp', 'tp'), may hold values from -6 to 6
- doc_start: int32 [256], replicated, may hold values from 0 to 255, as said below
- balanced_source: int32 [256], replicated, may hold values from 0 to 255, as said below
Outputs:
- mixed: bfloat16 [32768, 4096], P('cp', 'tp')
- query_grad: bfloat16 [32768, 4096], P('cp', 'tp')
- key_grad: bfloat16 [32768, 512], P('cp', 'tp')
- value_grad: bfloat16 [32768, 512], P('cp', 'tp')
Inputs may be any that keep to these rules, and one draw needn't show every extreme that they name: doc_start[b] is the first block of the document that holds block b; documents are runs of 1 to 8 consecutive blocks, one of them has exactly 8, and the last block is a document of one block. `balanced_source`: a permutation of the blocks that maps each aligned run of 16 blocks onto itself.
All inputs are finite; a program needn't handle non-finite values.
Results may differ from a plain program's by a relative error of at most 0.024.
Values may be sent and summed in bfloat16 or wider, within the bound.
No kernel may reach another device: no remote copies, remote signals or barrier semaphores. Data moves between devices by JAX's collectives and lax.ppermute only.
A program may use at most 128 MiB of HBM per device.

v0:
```python
import math

import jax
import jax.numpy as jnp
from jax import lax
from jax.experimental import pallas as pl
from jax.experimental.pallas import tpu as pltpu
from jax.sharding import PartitionSpec as P

HD = 128
BLOCK = 128
BLK_DEV = 4
MAXB = 8
GROUP = 4
PRIOR = MAXB - 1
POOL = PRIOR + BLK_DEV
ROWS = BLOCK * BLK_DEV
WIDTH = 1024
FAR_ROWS = (PRIOR - BLK_DEV) * BLOCK
CHUNKS = 2
CW = WIDTH // CHUNKS
FW = 512
BW = 512

SCALE = 1.0 / math.sqrt(HD)
SCALE_LOG2 = SCALE * math.log2(math.e)
MASKED = -1e30

START, GRAD_REL, GRAD_IDX, ATT_REL, ATT_IDX, CORE, TP = 0, 4, 8, 12, 16, 20, 21

ANY = pl.BlockSpec(memory_space=pl.ANY)
WHOLE = pl.BlockSpec(memory_space=pltpu.VMEM)
HBM = pl.BlockSpec(memory_space=pltpu.HBM)
SMEM = pl.BlockSpec(memory_space=pltpu.SMEM)
VMEM_LIMIT = 48 * 1024 * 1024


PARAMS = pltpu.CompilerParams(vmem_limit_bytes=VMEM_LIMIT)


def lasting(us):
    return pl.CostEstimate(
        flops=int(us * 1.15e9), bytes_accessed=int(us * 3.6e6), transcendentals=0
    )


def dot(a, b):
    return jnp.dot(a, b, preferred_element_type=jnp.float32)


def dot_nt(a, b):
    return lax.dot_general(a, b, (((1,), (1,)), ((), ())), preferred_element_type=jnp.float32)


def swap_cp(block, mask):
    count = lax.axis_size("cp")
    return lax.ppermute(block, "cp", [(i, i ^ mask) for i in range(count)])


def shift_cp(block, distance):
    count = lax.axis_size("cp")
    route = [(i, i + distance) for i in range(count) if 0 <= i + distance < count]
    return lax.ppermute(block, "cp", route)


def shift_tp(block, distance):
    count = lax.axis_size("tp")
    return lax.ppermute(block, "tp", [(i, (i + distance) % count) for i in range(count)])


def pool_copies(kv, far, near, keys, values, sems):
    copies = []
    for src, row, rows, place in (
        (kv, 0, ROWS, PRIOR * BLOCK),
        (far, 0, FAR_ROWS, 0),
        (near, 0, ROWS, ROWS - BLOCK),
    ):
        for col, pool in ((0, keys), (HD, values)):
            copies.append(
                pltpu.make_async_copy(
                    src.at[pl.ds(row, rows), pl.ds(col, HD)],
                    pool.at[pl.ds(place, rows)],
                    sems.at[len(copies)],
                )
            )
    return copies


def block_rows(b):
    return pl.ds(pl.multiple_of(b * BLOCK, BLOCK), BLOCK)


def first_mask(odd, width):
    key_pos = lax.broadcasted_iota(jnp.int32, (256, width), 0)
    row_pos = lax.broadcasted_iota(jnp.int32, (256, width), 1) % BLOCK + BLOCK
    return (key_pos <= row_pos) & (key_pos >= odd * BLOCK)


def flipped_heads(block):
    heads = block.shape[1] // HD
    return jnp.concatenate([block[:, h * HD : (h + 1) * HD].T for h in range(heads)], axis=1)


def stacked_heads(block):
    heads = block.shape[1] // HD
    return jnp.concatenate([block[:, h * HD : (h + 1) * HD] for h in range(heads)], axis=0)


def tiles_of(table, b):
    diag = PRIOR + b
    count = diag - jnp.maximum(table[START + b], 0) + 1
    return (count + 1) // 2, count % 2, diag


def low_of(step, odd, diag):
    block = diag - 1 - 2 * step + jnp.where(step > 0, odd, 0)
    return pl.multiple_of(block * BLOCK, BLOCK)


def forward_kernel(
    chunk, table, q_ref, *refs
):
    if chunk == 0:
        kv, far, near, att, att_t, total_ref, keys, values, sems = refs
        copies = pool_copies(kv, far, near, keys, values, sems)
        for copy in copies:
            copy.start()
        for copy in copies:
            copy.wait()
    else:
        keys, values, att, att_t, total_ref = refs

    groups = [slice(at, at + FW) for at in range(0, CW, FW)]

    def block(b, _):
        steps, odd, diag = tiles_of(table, b)
        q_t = [
            flipped_heads(q_ref[block_rows(b), chunk * CW + cols.start : chunk * CW + cols.stop])
            for cols in groups
        ]

        def tile(step, mask, carry):
            low = low_of(step, odd, diag)
            k = keys[pl.ds(low, 256), :]
            v_t = values[pl.ds(low, 256), :].T
            result = []
            for at in range(len(groups)):
                s = dot(k, q_t[at]) * SCALE_LOG2
                if carry is None:
                    s = jnp.where(mask, s, MASKED)
                    top = jnp.max(s, axis=0, keepdims=True)
                    p = jnp.exp2(s - top)
                    total = jnp.sum(p, axis=0, keepdims=True)
                    acc = dot(v_t, p.astype(jnp.bfloat16))
                else:
                    top_old, total, acc = carry[at]
                    top = jnp.maximum(top_old, jnp.max(s, axis=0, keepdims=True))
                    fade = jnp.exp2(top_old - top)
                    p = jnp.exp2(s - top)
                    total = total * fade + jnp.sum(p, axis=0, keepdims=True)
                    acc = acc * fade + dot(v_t, p.astype(jnp.bfloat16))
                result.append((top, total, acc))
            return result

        carry = tile(0, first_mask(odd, FW), None)
        carry = lax.fori_loop(1, steps, lambda step, carry: tile(step, None, carry), carry)
        for cols, (top, total, acc) in zip(groups, carry):
            out = (acc * (1.0 / total)).astype(jnp.bfloat16)
            att_t[b, :, cols] = out
            for head in range(FW // HD):
                at = cols.start + head * HD
                att[block_rows(b), at : at + HD] = out[:, head * HD : (head + 1) * HD].T
            total_ref[b, :, cols] = top + jnp.log2(total)
        return _

    lax.fori_loop(0, BLK_DEV, block, 0)


def forward(table, queries, pool, chunk):
    first = chunk == 0
    pool_shape = jax.ShapeDtypeStruct((POOL * BLOCK, HD), jnp.bfloat16)

    def kernel(*refs):
        forward_kernel(chunk, *refs)

    return pl.pallas_call(
        kernel,
        in_specs=[SMEM, WHOLE] + ([ANY] * 3 if first else [WHOLE] * 2),
        out_specs=[WHOLE] * (5 if first else 3),
        out_shape=[
            jax.ShapeDtypeStruct((ROWS, CW), jnp.bfloat16),
            jax.ShapeDtypeStruct((BLK_DEV, HD, CW), jnp.bfloat16),
            jax.ShapeDtypeStruct((BLK_DEV, 1, CW), jnp.float32),
        ]
        + ([pool_shape] * 2 if first else []),
        scratch_shapes=[pltpu.SemaphoreType.DMA((6,))] if first else [],
        compiler_params=PARAMS,
        cost_estimate=lasting(8),
        name="attention_forward",
    )(table, queries, *pool)


def start_chosen(rel, index, sources, place, sem, col=0):
    for at, source in enumerate(sources):
        @pl.when(rel == at)
        def _():
            pltpu.make_async_copy(
                source.at[pl.ds(pl.multiple_of(index * BLOCK, BLOCK), BLOCK)], place, sem
            ).start()


def backward_kernel(chunk, last, first, *refs):
    refs = list(refs)
    table, q_ref, att_t, total_ref, keys, values = refs[:6]
    sources = refs[6:10]
    refs = refs[10:]
    if not first:
        key_in, value_in = refs[1:3]
        refs = refs[3:]
    dq_hbm = refs[0]
    if last:
        own_ref, near_ref, far_ref = refs[1:4]
        refs = refs[4:]
        key_acc, value_acc = refs[:2]
    else:
        key_acc, value_acc = refs[1:3]
        refs = refs[3:]
    grads, dq, grad_sems, out_sems = refs[-4:]

    for at in range(BLK_DEV):
        start_chosen(
            table[GRAD_REL + at], table[GRAD_IDX + at], sources, grads.at[block_rows(at)], grad_sems.at[at]
        )
    key_acc[...] = jnp.zeros_like(key_acc)
    value_acc[...] = jnp.zeros_like(value_acc)
    for at in range(BLK_DEV):
        pltpu.make_async_copy(
            sources[0].at[pl.ds(0, BLOCK)], grads.at[block_rows(at)], grad_sems.at[at]
        ).wait()

    def outward(b):
        return pltpu.make_async_copy(
            dq.at[block_rows(b)], dq_hbm.at[block_rows(b), pl.ds(chunk * CW, CW)], out_sems.at[b]
        )

    groups = [slice(at, at + BW) for at in range(0, CW, BW)]

    def block(b, _):
        steps, odd, diag = tiles_of(table, b)
        held = []
        for cols in groups:
            q = q_ref[block_rows(b), chunk * CW + cols.start : chunk * CW + cols.stop]
            g = grads[block_rows(b), cols]
            g_t = flipped_heads(g)
            delta = jnp.sum(
                g_t.astype(jnp.float32) * att_t[b, :, cols].astype(jnp.float32),
                axis=0,
                keepdims=True,
            )
            held.append(
                (flipped_heads(q), stacked_heads(q), g_t, stacked_heads(g), delta, total_ref[b, :, cols])
            )

        def tile(step, mask, carry):
            low = low_of(step, odd, diag)
            k = keys[pl.ds(low, 256), :]
            k_t = k.T
            v = values[pl.ds(low, 256), :]
            result = []
            key_part = value_part = None
            for at, (q_t, q_s, g_t, g_s, delta, log_total) in enumerate(held):
                s = dot(k, q_t) * SCALE_LOG2
                if mask is not None:
                    s = jnp.where(mask, s, MASKED)
                p = jnp.exp2(s - log_total).astype(jnp.bfloat16)
                dp = dot(v, g_t)
                ds = (p.astype(jnp.float32) * (dp - delta)).astype(jnp.bfloat16)
                value_term, key_term, query_term = dot(p, g_s), dot(ds, q_s), dot(k_t, ds)
                value_part = value_term if value_part is None else value_part + value_term
                key_part = key_term if key_part is None else key_part + key_term
                result.append(query_term if carry is None else carry[at] + query_term)
            value_acc[pl.ds(low, 256), :] += value_part
            key_acc[pl.ds(low, 256), :] += key_part
            return result

        carry = tile(0, first_mask(odd, BW), None)
        carry = lax.fori_loop(1, steps, lambda step, carry: tile(step, None, carry), carry)
        for cols, dq_t in zip(groups, carry):
            dq_t = (dq_t * SCALE).astype(jnp.bfloat16)
            for head in range(BW // HD):
                at = cols.start + head * HD
                dq[block_rows(b), at : at + HD] = dq_t[:, head * HD : (head + 1) * HD].T
        outward(b).start()
        return _

    lax.fori_loop(0, BLK_DEV, block, 0)

    if last:
        near_at = ROWS - BLOCK
        own_at = PRIOR * BLOCK
        for acc, earlier, cols, factor in (
            (key_acc, key_in, slice(0, HD), SCALE),
            (value_acc, value_in, slice(HD, 2 * HD), 1.0),
        ):
            def total(rows):
                return (acc[rows] + earlier[rows]) * factor

            far_ref[:, cols] = total(slice(0, near_at)).astype(jnp.bfloat16)
            near_ref[:, cols] = total(slice(near_at, own_at)).astype(jnp.bfloat16)
            own_ref[:, cols] = total(slice(own_at, None))
    for b in range(BLK_DEV):
        outward(b).wait()


def backward(table, queries, att_t, totals, pool, sources, carried, chunk, last):
    first = carried is None
    pool_shape = (POOL * BLOCK, HD)
    sums = [jax.ShapeDtypeStruct(pool_shape, jnp.float32)] * 2
    if last:
        out_shape = [
            jax.ShapeDtypeStruct((ROWS, 2 * HD), jnp.float32),
            jax.ShapeDtypeStruct((ROWS, 2 * HD), jnp.bfloat16),
            jax.ShapeDtypeStruct((FAR_ROWS, 2 * HD), jnp.bfloat16),
        ]
        scratch = [pltpu.VMEM(pool_shape, jnp.float32)] * 2
    else:
        out_shape, scratch = sums, []

    def kernel(*refs):
        backward_kernel(chunk, last, first, *refs)

    return pl.pallas_call(
        kernel,
        in_specs=[SMEM] + [WHOLE] * 5 + [ANY] * 4 + ([] if first else [ANY, WHOLE, WHOLE]),
        out_specs=[ANY] + [WHOLE] * len(out_shape),
        out_shape=[jax.ShapeDtypeStruct((ROWS, WIDTH), jnp.bfloat16)] + out_shape,
        input_output_aliases={} if first else {10: 0},
        scratch_shapes=scratch
        + [
            pltpu.VMEM((ROWS, CW), jnp.bfloat16),
            pltpu.VMEM((ROWS, CW), jnp.bfloat16),
            pltpu.SemaphoreType.DMA((BLK_DEV,)),
            pltpu.SemaphoreType.DMA((BLK_DEV,)),
        ],
        compiler_params=PARAMS,
        cost_estimate=lasting(9),
        name="attention_backward",
    )(table, queries, att_t, totals, *pool, *sources, *([] if first else carried))


def grad_matmul_kernel(table, *refs):
    pieces, weight_hbm, outs = refs[:8], refs[8], refs[9 : 9 + CHUNKS]
    weight, sems = refs[9 + CHUNKS :]
    half = ROWS // 2
    copies = []
    for chunk in range(CHUNKS):
        for ahead in range(4):
            at = pl.multiple_of(((table[TP] + ahead) % 4) * WIDTH, WIDTH)
            copies.append(
                pltpu.make_async_copy(
                    weight_hbm.at[pl.ds(chunk * CW, CW), pl.ds(at, WIDTH)],
                    weight.at[4 * chunk + ahead],
                    sems.at[4 * chunk + ahead],
                )
            )
            copies[-1].start()
    for chunk in range(CHUNKS):
        totals = [None, None]
        for ahead in range(4):
            slot = 4 * chunk + ahead
            copies[slot].wait()
            for part in range(2):
                term = dot_nt(pieces[2 * ahead + part][...], weight[slot])
                totals[part] = term if totals[part] is None else totals[part] + term
        for part in range(2):
            outs[chunk][part * half : (part + 1) * half] = totals[part].astype(jnp.bfloat16)


def grad_matmul(table, pieces, weight):
    return pl.pallas_call(
        grad_matmul_kernel,
        in_specs=[SMEM] + [WHOLE] * 8 + [ANY],
        out_specs=[WHOLE] * CHUNKS,
        out_shape=[jax.ShapeDtypeStruct((ROWS, CW), jnp.bfloat16)] * CHUNKS,
        scratch_shapes=[
            pltpu.VMEM((4 * CHUNKS, CW, WIDTH), jnp.bfloat16),
            pltpu.SemaphoreType.DMA((4 * CHUNKS,)),
        ],
        compiler_params=PARAMS,
        cost_estimate=lasting(7),
        name="grad_projection",
    )(table, *pieces, weight)


HALF = WIDTH // 2


def weight_copy(table, weight_hbm, weight, slot, ahead, half, sem):
    at = pl.multiple_of(((table[TP] + ahead) % 4) * WIDTH + half * HALF, HALF)
    return pltpu.make_async_copy(weight_hbm.at[:, pl.ds(at, HALF)], weight.at[slot], sem)


def product_kernel(table, *refs):
    sources = [refs[4 * c : 4 * c + 4] for c in range(CHUNKS)]
    weight_hbm, left, right, onward, back, own, rows, weight, sems, weight_sems = refs[4 * CHUNKS :]

    def place(c, at):
        return rows.at[block_rows(at), pl.ds(c * CW, CW)]

    places = [(c, at, c * BLK_DEV + at) for c in range(CHUNKS) for at in range(BLK_DEV)]
    for c, at, sem in places:
        start_chosen(
            table[ATT_REL + at], table[ATT_IDX + at], sources[c], place(c, at), sems.at[sem]
        )
    parts = ((2, 0), (2, 1), (1, 1), (3, 0), (0, 0), (0, 1))
    weights = [
        weight_copy(table, weight_hbm, weight, slot, ahead, half, weight_sems.at[slot])
        for slot, (ahead, half) in enumerate(parts)
    ]
    for copy in weights:
        copy.start()
    for c, at, sem in places:
        pltpu.make_async_copy(sources[c][0].at[pl.ds(0, BLOCK)], place(c, at), sems.at[sem]).wait()
    for slot, out in enumerate((left, right, onward, back)):
        weights[slot].wait()
        out[...] = dot(rows[...], weight[slot]).astype(jnp.bfloat16)
    for slot in (4, 5):
        weights[slot].wait()
        own[:, (slot - 4) * HALF : (slot - 3) * HALF] = dot(rows[...], weight[slot]).astype(
            jnp.bfloat16
        )


def products(table, sources, weight):
    flat = [source for group in sources for source in group]
    return pl.pallas_call(
        product_kernel,
        in_specs=[SMEM] + [ANY] * (4 * CHUNKS + 1),
        out_specs=[WHOLE] * 6,
        out_shape=[jax.ShapeDtypeStruct((ROWS, HALF), jnp.bfloat16)] * 4
        + [jax.ShapeDtypeStruct((ROWS, WIDTH), jnp.bfloat16)] * 2,
        scratch_shapes=[
            pltpu.VMEM((6, WIDTH, HALF), jnp.bfloat16),
            pltpu.SemaphoreType.DMA((4 * CHUNKS,)),
            pltpu.SemaphoreType.DMA((6,)),
        ],
        compiler_params=PARAMS,
        cost_estimate=lasting(7),
        name="products",
    )(table, *flat, weight)


def sum_product_kernel(table, rows, weight_hbm, before, after_, onward, back, weight, sems):
    weights = [
        weight_copy(table, weight_hbm, weight, 0, 1, 0, sems.at[0]),
        weight_copy(table, weight_hbm, weight, 1, 3, 1, sems.at[1]),
    ]
    for copy in weights:
        copy.start()
    for slot, (extra, out) in enumerate(((before, onward), (after_, back))):
        weights[slot].wait()
        value = dot(rows[...], weight[slot])
        out[...] = (value + extra[...].astype(jnp.float32)).astype(jnp.bfloat16)


def sum_products(table, rows, weight, before, after):
    half = jax.ShapeDtypeStruct((ROWS, HALF), jnp.bfloat16)
    return pl.pallas_call(
        sum_product_kernel,
        in_specs=[SMEM, WHOLE, ANY, WHOLE, WHOLE],
        out_specs=[WHOLE] * 2,
        out_shape=[half] * 2,
        scratch_shapes=[
            pltpu.VMEM((2, WIDTH, HALF), jnp.bfloat16),
            pltpu.SemaphoreType.DMA((2,)),
        ],
        compiler_params=PARAMS,
        cost_estimate=lasting(4),
        name="sum_products",
    )(table, rows, weight, before, after)


def last_sum_kernel(own, before_a, before_b, after_a, after_b, out):
    for half, before, after in ((0, before_a, after_a), (1, before_b, after_b)):
        cols = slice(half * 512, (half + 1) * 512)
        out[:, cols] = (
            own[:, cols].astype(jnp.float32) + before[...].astype(jnp.float32) + after[...].astype(jnp.float32)
        ).astype(jnp.bfloat16)


def last_sum(own, before_a, before_b, after_a, after_b):
    part = pl.BlockSpec((BLOCK, 512), lambda j: (j, 0))
    full = pl.BlockSpec((BLOCK, WIDTH), lambda j: (j, 0))
    return pl.pallas_call(
        last_sum_kernel,
        grid=(4,),
        in_specs=[full, part, part, part, part],
        out_specs=full,
        out_shape=jax.ShapeDtypeStruct((ROWS, WIDTH), jnp.bfloat16),
        compiler_params=PARAMS,
        cost_estimate=lasting(2),
        name="last_sum",
    )(own, before_a, before_b, after_a, after_b)


def scalar_table(doc_start, balanced_source):
    device = lax.axis_index("cp")
    member = device % GROUP
    group_blocks = GROUP * BLK_DEV
    group_first = device // GROUP * group_blocks
    sources = lax.dynamic_slice_in_dim(balanced_source, group_first, group_blocks) - group_first
    slots = jnp.arange(group_blocks, dtype=jnp.int32)
    slot_of = jnp.sum(
        jnp.where(sources[None, :] == slots[:, None], slots[None, :], 0), axis=1, dtype=jnp.int32
    )
    mine = member * BLK_DEV
    wanted = lax.dynamic_slice_in_dim(sources, mine, BLK_DEV)
    held = lax.dynamic_slice_in_dim(slot_of, mine, BLK_DEV)
    starts = lax.dynamic_slice_in_dim(doc_start, device * BLK_DEV, BLK_DEV)
    starts = starts - (device * BLK_DEV - PRIOR)
    return jnp.concatenate(
        [
            starts,
            (held // BLK_DEV) ^ member,
            held % BLK_DEV,
            (wanted // BLK_DEV) ^ member,
            wanted % BLK_DEV,
            jnp.stack([device % 2, lax.axis_index("tp")]),
        ]
    ).astype(jnp.int32)


def group_exchange(block, earlier):
    across = swap_cp(block, 2)
    return [block, swap_cp(after(block, earlier), 1), across, swap_cp(after(across, earlier), 1)]


def copy_all(*pairs, sems):
    copies = [pltpu.make_async_copy(src, dst, sems.at[at]) for at, (src, dst) in enumerate(pairs)]
    for copy in copies:
        copy.start()
    for copy in copies:
        copy.wait()


def join_kernel(keys, values, grads, kv, last, upper, lower, sems):
    half = ROWS // 2
    tail = pl.ds(ROWS - FAR_ROWS, FAR_ROWS)
    left, right = pl.ds(0, HD), pl.ds(HD, HD)
    copy_all(
        (keys, kv.at[:, left]),
        (values, kv.at[:, right]),
        (keys.at[tail], last.at[:, left]),
        (values.at[tail], last.at[:, right]),
        (grads.at[pl.ds(0, half)], upper),
        (grads.at[pl.ds(half, half)], lower),
        sems=sems,
    )


def join(keys, values, grads):
    return pl.pallas_call(
        join_kernel,
        in_specs=[HBM] * 3,
        out_specs=[WHOLE] * 4,
        out_shape=[
            jax.ShapeDtypeStruct((ROWS, 2 * HD), jnp.bfloat16),
            jax.ShapeDtypeStruct((FAR_ROWS, 2 * HD), jnp.bfloat16),
        ]
        + [jax.ShapeDtypeStruct((ROWS // 2, WIDTH), jnp.bfloat16)] * 2,
        scratch_shapes=[pltpu.SemaphoreType.DMA((6,))],
        compiler_params=PARAMS,
        cost_estimate=lasting(2),
        name="join",
    )(keys, values, grads)


def add_kernel(own, near, far, keys, values):
    total = own[...] + near[...].astype(jnp.float32)
    front = total[: ROWS - FAR_ROWS].astype(jnp.bfloat16)
    rear = (total[ROWS - FAR_ROWS :] + far[...].astype(jnp.float32)).astype(jnp.bfloat16)
    for col, out in ((0, keys), (HD, values)):
        out[: ROWS - FAR_ROWS] = front[:, col : col + HD]
        out[ROWS - FAR_ROWS :] = rear[:, col : col + HD]


def add_terms(own, near, far):
    return pl.pallas_call(
        add_kernel,
        in_specs=[WHOLE] * 3,
        out_specs=[WHOLE] * 2,
        out_shape=[jax.ShapeDtypeStruct((ROWS, HD), jnp.bfloat16)] * 2,
        compiler_params=PARAMS,
        cost_estimate=lasting(1),
        name="add_terms",
    )(own, near, far)


def after(value, earlier):
    return lax.optimization_barrier((value, earlier))[0]


def shards(queries, key_rows, value_rows, out_proj, grad_mixed, doc_start, balanced_source):
    table = scalar_table(doc_start, balanced_source)

    kv, last, upper, lower = join(key_rows, value_rows, grad_mixed)
    far = shift_cp(last, 2)
    near = shift_cp(kv, 1)
    pool = (kv, far, near)

    before_upper = shift_tp(upper, 1)
    ahead_lower = shift_tp(lower, -1)
    before_lower = shift_tp(after(lower, far), 1)
    ahead_upper = shift_tp(after(upper, far), -1)

    attended, attended_t, totals = [], [], []
    for chunk in range(CHUNKS):
        att, att_t, total, *laid_out = forward(
            after(table, (attended[0], before_upper, ahead_lower))
            if chunk
            else table,
            queries,
            pool,
            chunk,
        )
        if chunk == 0:
            pool = laid_out
            opposite = [
                shift_tp(after(before_upper, att), 1),
                shift_tp(after(ahead_lower, att), -1),
            ]
        attended.append(att)
        attended_t.append(att_t)
        totals.append(total)

    pieces = (upper, lower, ahead_upper, ahead_lower, *opposite, before_upper, before_lower)
    exchanged = [group_exchange(attended[0], attended[1]), None]
    grad_attended = grad_matmul(table, pieces, out_proj)
    across = swap_cp(after(attended[1], (before_lower, ahead_upper)), 2)
    exchanged[1] = [
        attended[1],
        swap_cp(after(attended[1], grad_attended[1]), 1),
        across,
        swap_cp(after(across, grad_attended[1]), 1),
    ]
    grad_across = swap_cp(grad_attended[0], 2)

    far_left, far_right, onward_b, back_a, own, rows = products(
        after(table, grad_attended[1]), exchanged, out_proj
    )
    from_before = shift_tp(far_left, 1)
    from_after = shift_tp(far_right, -1)

    grad_sources = [
        [
            grad_attended[0],
            swap_cp(after(grad_attended[0], own), 1),
            grad_across,
            swap_cp(after(grad_across, own), 1),
        ]
    ]
    swapped = swap_cp(grad_attended[1], 1)
    carried = backward(
        after(table, (own, swapped)),
        queries, attended_t[0], totals[0], pool, grad_sources[0], None, 0, False,
    )
    query_a = carried[1]
    across = swap_cp(after(grad_attended[1], grad_across), 2)
    grad_sources.append(
        [
            grad_attended[1],
            swapped,
            across,
            swap_cp(after(across, query_a), 1),
        ]
    )
    before_b = shift_tp(onward_b, 1)
    after_a = shift_tp(back_a, -1)
    onward_a, back_b = sum_products(
        after(table, query_a), rows, out_proj, from_before, from_after)
    before_a = shift_tp(onward_a, 1)
    after_b = shift_tp(back_b, -1)
    query_grad, own_grads, near_grads, far_grads = backward(
        after(table, onward_a),
        queries, attended_t[1], totals[1], pool, grad_sources[1], carried, 1, True,
    )
    far_back = shift_cp(after(far_grads, (before_b, after_a)), -2)
    near_back = shift_cp(after(near_grads, (before_b, after_a)), -1)
    mixed = last_sum(own, before_a, before_b, after_a, after_b)
    key_grad, value_grad = add_terms(after(own_grads, mixed), near_back, far_back)
    return (mixed, query_grad, key_grad, value_grad)


def solution(mesh):
    placed = (P("cp", "tp"), P("cp", "tp"), P("cp", "tp"), P("tp", None), P("cp", "tp"), P(), P())
    return jax.shard_map(
        shards,
        mesh=mesh,
        in_specs=placed,
        out_specs=(P("cp", "tp"),) * 4,
        check_vma=False,
    )
```

profile of v0, /device:TPU:64, one launch (start us, length us, event | category | flops | bytes accessed | tf_op | source)
XLA Modules:
  0.0 122.1 jit_solution(8028209450084979751)
XLA Ops:
  0.6 1.2 copy-done
  1.9 0.9 copy-done.2
  2.8 0.9 copy-done.3
  3.7 0.9 join.1
  4.6 3.8 %collective-permute-start = (bf16[384,256]{1,0:T(8,128)(2,1)}, bf16[384,256]{1,0:T(8,128)(2,1)}, u32[]{:S(2)}, u32[]{:S(2)}) collective-permute-start(bf16[384,256]{1,0:T(8,128)(2,1)} %get-tuple-element.58), channel_id=1, source_target_pairs={{0,8},{4,12},{8,16},{12,20},{16,24},{20,28},{24,32},{28,36},{32,40... | collective-permute-start | bytes 589832 | tf_op jit(solution)/shard_map/ppermute | solution.py:63
  8.4 1.9 %collective-permute-start.4 = (bf16[512,256]{1,0:T(8,128)(2,1)S(1)}, bf16[512,256]{1,0:T(8,128)(2,1)}, u32[]{:S(2)}, u32[]{:S(2)}) collective-permute-start(bf16[512,256]{1,0:T(8,128)(2,1)S(1)} %get-tuple-element.60.refs_2_), channel_id=1, source_target_pairs={{0,4},{4,8},{8,12},{12,16},{16,20},{20,24},{24,28},{28,32},{32,36}... | collective-permute-start | bytes 786440 | tf_op jit(solution)/shard_map/ppermute | solution.py:63
  10.3 2.8 %collective-permute-start.2 = (bf16[256,1024]{1,0:T(8,128)(2,1)S(1)}, bf16[256,1024]{1,0:T(8,128)(2,1)S(1)}, u32[]{:S(2)}, u32[]{:S(2)}) collective-permute-start(bf16[256,1024]{1,0:T(8,128)(2,1)S(1)} %get-tuple-element.64.refs_1_), channel_id=1, source_target_pairs={{0,3},{1,0},{2,1},{3,2},{4,7},{5,4},{6,5},{7,6},{8,11},{9,8},{10,9... | collective-permute-start | bytes 1572872 | tf_op jit(solution)/shard_map/ppermute | solution.py:68
  13.2 0.0 collective-permute-start.3
  13.2 0.1 dynamic-slice_subtract_fusion
  13.3 0.1 select_reduce_fusion
  13.4 0.1 and_select_fusion
  13.5 0.1 and_select_fusion.2
  13.5 0.1 dynamic-slice_subtract_fusion.1
  13.6 0.1 fusion
  13.7 0.1 concatenate.3.refs_0_.table
  13.8 0.0 collective-permute-done.refs_3_
  13.8 1.1 collective-permute-start.7
  14.9 2.3 %collective-permute-start.1 = (bf16[256,1024]{1,0:T(8,128)(2,1)S(1)}, bf16[256,1024]{1,0:T(8,128)(2,1)S(1)}, u32[]{:S(2)}, u32[]{:S(2)}) collective-permute-start(bf16[256,1024]{1,0:T(8,128)(2,1)S(1)} %get-tuple-element.59.refs_0_), channel_id=1, source_target_pairs={{0,3},{1,0},{2,1},{3,2},{4,7},{5,4},{6,5},{7,6},{8,11},{9,8},{10,9... | collective-permute-start | bytes 1572872 | tf_op jit(solution)/shard_map/ppermute | solution.py:68
  17.2 5.9 %attention_forward.2 = (bf16[512,512]{1,0:T(8,128)(2,1)S(1)}, bf16[4,128,512]{2,1,0:T(8,128)(2,1)S(1)}, f32[4,1,512]{2,1,0:T(1,128)S(1)}, bf16[1408,128]{1,0:T(8,128)(2,1)S(1)}, bf16[1408,128]{1,0:T(8,128)(2,1)S(1)}) custom-call(s32[22]{0:T(128)S(1)} %concatenate.3.refs_0_.table, bf16[512,1024]{1,0:T(8,128)(2,1)S(1)} %copy-done.1, ...), custom_call_target="tpu_custom_call" | custom-call | flops 9200000000 | bytes 28800000 | tf_op jit(solution)/shard_map/attention_forward/pallas_call | solution.py:186
  23.1 0.8 copy-done.8
  23.9 5.7 %collective-permute-start.9 = (bf16[512,512]{1,0:T(8,128)(2,1)S(1)}, bf16[512,512]{1,0:T(8,128)(2,1)S(1)}, u32[]{:S(2)}, u32[]{:S(2)}) collective-permute-start(bf16[512,512]{1,0:T(8,128)(2,1)S(1)} %get-tuple-element.71.refs_0_), channel_id=1, source_target_pairs={{0,8},{4,12},{8,0},{12,4},{16,24},{20,28},{24,16},{28,20},{32,40},... | collective-permute-start | bytes 1572872 | tf_op jit(solution)/shard_map/ppermute | solution.py:57
  29.6 0.0 collective-permute-done.2.refs_3_
  29.6 0.0 collective-permute-done.3.refs_6_
  29.6 1.9 %collective-permute-start.6 = (bf16[256,1024]{1,0:T(8,128)(2,1)S(1)}, bf16[256,1024]{1,0:T(8,128)(2,1)S(1)}, u32[]{:S(2)}, u32[]{:S(2)}) collective-permute-start(bf16[256,1024]{1,0:T(8,128)(2,1)S(1)} %collective-permute-done.2.refs_3_), channel_id=1, source_target_pairs={{0,3},{1,0},{2,1},{3,2},{4,7},{5,4},{6,5},{7,6},{8,11},{9,8},{10,9... | collective-permute-start | bytes 1572872 | tf_op jit(solution)/shard_map/ppermute | solution.py:68
  31.5 0.1 collective-permute-start.5
  31.6 4.7 %attention_forward.3 = (bf16[512,512]{1,0:T(8,128)(2,1)S(1)}, bf16[4,128,512]{2,1,0:T(8,128)(2,1)S(1)}, f32[4,1,512]{2,1,0:T(1,128)S(1)}) custom-call(s32[22]{0:T(128)S(1)} %concatenate.3.refs_0_.table, bf16[512,1024]{1,0:T(8,128)(2,1)S(1)} %copy-done.1, bf16[1408,128]{1,0:T(8,128)(2,1)S(1)} %get-tuple-element.68.refs_2_.refs_4_, ...), custom_call_target="tpu_custom_call" | custom-call | flops 9200000000 | bytes 28800000 | tf_op jit(solution)/shard_map/attention_forward/pallas_call | solution.py:186
  36.4 0.8 copy-done.6
  37.2 1.2 collective-permute-done.7.refs_7_
  38.4 4.2 %collective-permute-start.8 = (bf16[512,512]{1,0:T(8,128)(2,1)S(1)}, bf16[512,512]{1,0:T(8,128)(2,1)S(1)}, u32[]{:S(2)}, u32[]{:S(2)}) collective-permute-start(bf16[512,512]{1,0:T(8,128)(2,1)S(1)} %get-tuple-element.71.refs_0_), channel_id=1, source_target_pairs={{0,4},{4,0},{8,12},{12,8},{16,20},{20,16},{24,28},{28,24},{32,36},... | collective-permute-start | bytes 1572872 | tf_op jit(solution)/shard_map/ppermute | solution.py:57
  42.6 1.0 collective-permute-start.12
  43.6 0.2 collective-permute-start.10
  43.8 1.8 %collective-permute-done.6.refs_5_ = bf16[256,1024]{1,0:T(8,128)(2,1)S(1)} collective-permute-done((bf16[256,1024]{1,0:T(8,128)(2,1)S(1)}, bf16[256,1024]{1,0:T(8,128)(2,1)S(1)}, u32[]{:S(2)}, u32[]{:S(2)}) %collective-permute-start.6) | collective-permute-done | bytes 524320 | tf_op jit(solution)/shard_map/ppermute | solution.py:68
  45.6 4.0 %collective-permute-done.5.refs_4_ = bf16[256,1024]{1,0:T(8,128)(2,1)S(1)} collective-permute-done((bf16[256,1024]{1,0:T(8,128)(2,1)S(1)}, bf16[256,1024]{1,0:T(8,128)(2,1)S(1)}, u32[]{:S(2)}, u32[]{:S(2)}) %collective-permute-start.5) | collective-permute-done | bytes 524320 | tf_op jit(solution)/shard_map/ppermute | solution.py:68
  49.6 7.5 %grad_projection.1 = (bf16[512,512]{1,0:T(8,128)(2,1)S(1)}, bf16[512,512]{1,0:T(8,128)(2,1)S(1)}) custom-call(s32[22]{0:T(128)S(1)} %concatenate.3.refs_0_.table, bf16[256,1024]{1,0:T(8,128)(2,1)S(1)} %get-tuple-element.59.refs_0_, bf16[256,1024]{1,0:T(8,128)(2,1)S(1)} %get-tuple-element.64.refs_1_, bf16[256,1024]{1,0:T(8,128)(2,1)S(1)} %collective-permute-done.1.refs_2_, ...), custom_call_target="tpu_custom_call" | custom-call | flops 8049999872 | bytes 25200000 | tf_op jit(solution)/shard_map/grad_projection/pallas_call | solution.py:380
  57.1 2.0 %collective-permute-start.11 = (bf16[512,512]{1,0:T(8,128)(2,1)S(1)}, bf16[512,512]{1,0:T(8,128)(2,1)S(1)}, u32[]{:S(2)}, u32[]{:S(2)}) collective-permute-start(bf16[512,512]{1,0:T(8,128)(2,1)S(1)} %get-tuple-element.74.refs_4_), channel_id=1, source_target_pairs={{0,4},{4,0},{8,12},{12,8},{16,20},{20,16},{24,28},{28,24},{32,36},... | collective-permute-start | bytes 1572872 | tf_op jit(solution)/shard_map/ppermute | solution.py:57
  59.0 0.0 collective-permute-done.12.refs_6_
  59.1 0.1 collective-permute-start.13
  59.2 0.4 collective-permute-start.14
  59.6 0.0 collective-permute-done.8.refs_1_
  59.6 3.4 %collective-permute-start.16 = (bf16[512,512]{1,0:T(8,128)(2,1)S(1)}, bf16[512,512]{1,0:T(8,128)(2,1)S(1)}, u32[]{:S(2)}, u32[]{:S(2)}) collective-permute-start(bf16[512,512]{1,0:T(8,128)(2,1)S(1)} %get-tuple-element.81.refs_6_), channel_id=1, source_target_pairs={{0,8},{4,12},{8,0},{12,4},{16,24},{20,28},{24,16},{28,20},{32,40},... | collective-permute-start | bytes 1572872 | tf_op jit(solution)/shard_map/ppermute | solution.py:57
  63.0 0.0 collective-permute-done.13.refs_7_
  63.0 0.0 copy-start.16
  63.0 0.8 copy-done.16
  63.8 7.5 %products.1 = (bf16[512,512]{1,0:T(8,128)(2,1)S(1)}, bf16[512,512]{1,0:T(8,128)(2,1)S(1)}, bf16[512,512]{1,0:T(8,128)(2,1)S(1)}, bf16[512,512]{1,0:T(8,128)(2,1)...) custom-call(s32[22]{0:T(128)S(1)} %concatenate.3.refs_0_.table, ...), custom_call_target="tpu_custom_call" | custom-call | flops 8049999872 | bytes 25200000 | tf_op jit(solution)/shard_map/products/pallas_call | solution.py:436
  71.2 4.2 %collective-permute-done.16.refs_8_ = bf16[512,512]{1,0:T(8,128)(2,1)S(1)} collective-permute-done((bf16[512,512]{1,0:T(8,128)(2,1)S(1)}, bf16[512,512]{1,0:T(8,128)(2,1)S(1)}, u32[]{:S(2)}, u32[]{:S(2)}) %collective-permute-start.16) | collective-permute-done | bytes 524320 | tf_op jit(solution)/shard_map/ppermute | solution.py:57
  75.4 0.0 collective-permute-start.17
  75.4 0.5 collective-permute-start.15
  76.0 1.8 %collective-permute-start.24 = (bf16[512,512]{1,0:T(8,128)(2,1)S(1)}, bf16[512,512]{1,0:T(8,128)(2,1)S(1)}, u32[]{:S(2)}, u32[]{:S(2)}) collective-permute-start(bf16[512,512]{1,0:T(8,128)(2,1)S(1)} %get-tuple-element.95.refs_6_), channel_id=1, source_target_pairs={{0,8},{4,12},{8,0},{12,4},{16,24},{20,28},{24,16},{28,20},{32,40},... | collective-permute-start | bytes 1572872 | tf_op jit(solution)/shard_map/ppermute | solution.py:57
  77.7 0.0 collective-permute-done.14.refs_7_
  77.7 0.0 collective-permute-start.18
  77.7 3.2 %collective-permute-start.19 = (bf16[512,512]{1,0:T(8,128)(2,1)S(1)}, bf16[512,512]{1,0:T(8,128)(2,1)S(1)}, u32[]{:S(2)}, u32[]{:S(2)}) collective-permute-start(bf16[512,512]{1,0:T(8,128)(2,1)S(1)} %get-tuple-element.87), channel_id=1, source_target_pairs={{0,3},{1,0},{2,1},{3,2},{4,7},{5,4},{6,5},{7,6},{8,11},{9,8},{10,9... | collective-permute-start | bytes 1572872 | tf_op jit(solution)/shard_map/ppermute | solution.py:68
  81.0 6.4 %attention_backward.2 = (bf16[512,1024]{1,0:T(8,128)(2,1)}, f32[1408,128]{1,0:T(8,128)S(1)}, f32[1408,128]{1,0:T(8,128)S(1)}) custom-call(s32[22]{0:T(128)S(1)} %concatenate.3.refs_0_.table, bf16[512,1024]{1,0:T(8,128)(2,1)S(1)} %copy-done.1, bf16[4,128,512]{2,1,0:T(8,128)(2,1)S(1)} %copy-done.9, f32[4,1,512]{2,1,0:T(1,128)S(1)} %get-tuple-element.79.refs_3_, ...), custom_call_target="tpu_custom_call" | custom-call | flops 10350000128 | bytes 32400000 | tf_op jit(solution)/shard_map/attention_backward/pallas_call | solution.py:332
  87.4 2.4 %collective-permute-done.24.refs_8_ = bf16[512,512]{1,0:T(8,128)(2,1)S(1)} collective-permute-done((bf16[512,512]{1,0:T(8,128)(2,1)S(1)}, bf16[512,512]{1,0:T(8,128)(2,1)S(1)}, u32[]{:S(2)}, u32[]{:S(2)}) %collective-permute-start.24) | collective-permute-done | bytes 524320 | tf_op jit(solution)/shard_map/ppermute | solution.py:57
  89.8 3.2 %collective-permute-start.22 = (bf16[512,512]{1,0:T(8,128)(2,1)S(1)}, bf16[512,512]{1,0:T(8,128)(2,1)S(1)}, u32[]{:S(2)}, u32[]{:S(2)}) collective-permute-start(bf16[512,512]{1,0:T(8,128)(2,1)S(1)} %get-tuple-element.90), channel_id=1, source_target_pairs={{0,3},{1,0},{2,1},{3,2},{4,7},{5,4},{6,5},{7,6},{8,11},{9,8},{10,9... | collective-permute-start | bytes 1572872 | tf_op jit(solution)/shard_map/ppermute | solution.py:68
  93.1 3.2 %sum_products.1 = (bf16[512,512]{1,0:T(8,128)(2,1)S(1)}, bf16[512,512]{1,0:T(8,128)(2,1)S(1)}) custom-call(s32[22]{0:T(128)S(1)} %concatenate.3.refs_0_.table, bf16[512,1024]{1,0:T(8,128)(2,1)S(1)} %copy-done.5, bf16[1024,4096]{1,0:T(8,128)(2,1)} %weight_hbm.1, bf16[512,512]{1,0:T(8,128)(2,1)S(1)} %collective-permute-done.18.before, ...), custom_call_target="tpu_custom_call" | custom-call | flops 4600000000 | bytes 14400000 | tf_op jit(solution)/shard_map/sum_products/pallas_call | solution.py:468
  96.3 0.1 collective-permute-start.20
  96.4 3.2 %collective-permute-start.23 = (bf16[512,512]{1,0:T(8,128)(2,1)S(1)}, bf16[512,512]{1,0:T(8,128)(2,1)S(1)}, u32[]{:S(2)}, u32[]{:S(2)}) collective-permute-start(bf16[512,512]{1,0:T(8,128)(2,1)S(1)} %get-tuple-element.91), channel_id=1, source_target_pairs={{0,3},{1,0},{2,1},{3,2},{4,7},{5,4},{6,5},{7,6},{8,11},{9,8},{10,9... | collective-permute-start | bytes 1572872 | tf_op jit(solution)/shard_map/ppermute | solution.py:68
  99.6 7.1 %attention_backward.3 = (bf16[512,1024]{1,0:T(8,128)(2,1)}, f32[512,256]{1,0:T(8,128)S(1)}, bf16[512,256]{1,0:T(8,128)(2,1)S(1)}, bf16[384,256]{1,0:T(8,128)(2,1)S(1)}) custom-call(s32[22]{0:T(128)S(1)} %concatenate.3.refs_0_.table, bf16[512,1024]{1,0:T(8,128)(2,1)} %refs_1_.7, bf16[4,128,512]{2,1,0:T(8,128)(2,1)S(1)} %copy-done.7, ...), custom_call_target="tpu_custom_call", output_to_operand_aliasing={{0}: (10, {})} | custom-call | flops 10350000128 | bytes 32400000 | tf_op jit(solution)/shard_map/attention_backward/pallas_call | solution.py:332
  106.8 1.9 %collective-permute-start.26 = (bf16[512,256]{1,0:T(8,128)(2,1)S(1)}, bf16[512,256]{1,0:T(8,128)(2,1)S(1)}, u32[]{:S(2)}, u32[]{:S(2)}) collective-permute-start(bf16[512,256]{1,0:T(8,128)(2,1)S(1)} %get-tuple-element.103), channel_id=1, source_target_pairs={{4,0},{8,4},{12,8},{16,12},{20,16},{24,20},{28,24},{32,28},{36,32}... | collective-permute-start | bytes 786440 | tf_op jit(solution)/shard_map/ppermute | solution.py:63
  108.7 1.9 %collective-permute-start.27 = (bf16[384,256]{1,0:T(8,128)(2,1)S(1)}, bf16[384,256]{1,0:T(8,128)(2,1)S(1)}, u32[]{:S(2)}, u32[]{:S(2)}) collective-permute-start(bf16[384,256]{1,0:T(8,128)(2,1)S(1)} %get-tuple-element.105), channel_id=1, source_target_pairs={{8,0},{12,4},{16,8},{20,12},{24,16},{28,20},{32,24},{36,28},{40,32... | collective-permute-start | bytes 589832 | tf_op jit(solution)/shard_map/ppermute | solution.py:63
  110.6 5.9 %collective-permute-done.20.before_a = bf16[512,512]{1,0:T(8,128)(2,1)S(1)} collective-permute-done((bf16[512,512]{1,0:T(8,128)(2,1)S(1)}, bf16[512,512]{1,0:T(8,128)(2,1)S(1)}, u32[]{:S(2)}, u32[]{:S(2)}) %collective-permute-start.20) | collective-permute-done | bytes 524320 | tf_op jit(solution)/shard_map/ppermute | solution.py:68
  116.6 1.7 %last_sum.1 = bf16[512,1024]{1,0:T(8,128)(2,1)} custom-call(bf16[512,1024]{1,0:T(8,128)(2,1)S(1)} %copy-done.4, bf16[512,512]{1,0:T(8,128)(2,1)S(1)} %collective-permute-done.20.before_a, bf16[512,512]{1,0:T(8,128)(2,1)S(1)} %collective-permute-done.21.before_b, bf16[512,512]{1,0:T(8,128)(2,1)S(1)} %collective-permute-done.22.after_a, ...), custom_call_target="tpu_custom_call" | custom-call | flops 2300000000 | bytes 7200000 | tf_op jit(solution)/shard_map/last_sum/pallas_call | solution.py:494
  118.3 3.1 %collective-permute-done.27.far = bf16[384,256]{1,0:T(8,128)(2,1)S(1)} collective-permute-done((bf16[384,256]{1,0:T(8,128)(2,1)S(1)}, bf16[384,256]{1,0:T(8,128)(2,1)S(1)}, u32[]{:S(2)}, u32[]{:S(2)}) %collective-permute-start.27) | collective-permute-done | bytes 196640 | tf_op jit(solution)/shard_map/ppermute | solution.py:63
  121.4 0.8 add_terms.1
  (43 shorter events, 0.1 us)
Async XLA Ops:
  0.6 1.2 %copy-start = (bf16[512,1024]{1,0:T(8,128)(2,1)S(1)}, bf16[512,1024]{1,0:T(8,128)(2,1)}, u32[]{:S(2)}) copy-start(bf16[512,1024]{1,0:T(8,128)(2,1)} %grads.1) | copy-start | bytes 3145732
  1.9 0.9 copy-start.2
  2.8 0.9 copy-start.3
  3.7 9.5 %copy-start.14 = (s32[256]{0:T(256)S(1)}, s32[256]{0:T(256)}, u32[]{:S(2)}) copy-start(s32[256]{0:T(256)} %param.13) | copy-start | bytes 3076
  3.7 9.9 %copy-start.15 = (s32[256]{0:T(256)S(1)}, s32[256]{0:T(256)}, u32[]{:S(2)}) copy-start(s32[256]{0:T(256)} %param.12) | copy-start | bytes 3076
  3.7 13.5 %copy-start.1 = (bf16[512,1024]{1,0:T(8,128)(2,1)S(1)}, bf16[512,1024]{1,0:T(8,128)(2,1)}, u32[]{:S(2)}) copy-start(bf16[512,1024]{1,0:T(8,128)(2,1)} %refs_1_.7) | copy-start | bytes 3145732
  4.6 9.2 %collective-permute-start = (bf16[384,256]{1,0:T(8,128)(2,1)}, bf16[384,256]{1,0:T(8,128)(2,1)}, u32[]{:S(2)}, u32[]{:S(2)}) collective-permute-start(bf16[384,256]{1,0:T(8,128)(2,1)} %get-tuple-element.58), channel_id=1, source_target_pairs={{0,8},{4,12},{8,16},{12,20},{16,24},{20,28},{24,32},{28,36},{32,40... | collective-permute-start | bytes 589832 | tf_op jit(solution)/shard_map/ppermute | solution.py:63
  8.4 8.8 %collective-permute-start.4 = (bf16[512,256]{1,0:T(8,128)(2,1)S(1)}, bf16[512,256]{1,0:T(8,128)(2,1)}, u32[]{:S(2)}, u32[]{:S(2)}) collective-permute-start(bf16[512,256]{1,0:T(8,128)(2,1)S(1)} %get-tuple-element.60.refs_2_), channel_id=1, source_target_pairs={{0,4},{4,8},{8,12},{12,16},{16,20},{20,24},{24,28},{28,32},{32,36}... | collective-permute-start | bytes 786440 | tf_op jit(solution)/shard_map/ppermute | solution.py:63
  10.3 19.2 %collective-permute-start.2 = (bf16[256,1024]{1,0:T(8,128)(2,1)S(1)}, bf16[256,1024]{1,0:T(8,128)(2,1)S(1)}, u32[]{:S(2)}, u32[]{:S(2)}) collective-permute-start(bf16[256,1024]{1,0:T(8,128)(2,1)S(1)} %get-tuple-element.64.refs_1_), channel_id=1, source_target_pairs={{0,3},{1,0},{2,1},{3,2},{4,7},{5,4},{6,5},{7,6},{8,11},{9,8},{10,9... | collective-permute-start | bytes 1572872 | tf_op jit(solution)/shard_map/ppermute | solution.py:68
  13.2 16.4 %collective-permute-start.3 = (bf16[256,1024]{1,0:T(8,128)(2,1)S(1)}, bf16[256,1024]{1,0:T(8,128)(2,1)S(1)}, u32[]{:S(2)}, u32[]{:S(2)}) collective-permute-start(bf16[256,1024]{1,0:T(8,128)(2,1)S(1)} %get-tuple-element.59.refs_0_), channel_id=1, source_target_pairs={{0,1},{1,2},{2,3},{3,0},{4,5},{5,6},{6,7},{7,4},{8,9},{9,10},{10,1... | collective-permute-start | bytes 1572872 | tf_op jit(solution)/shard_map/ppermute | solution.py:68
  13.8 24.6 %collective-permute-start.7 = (bf16[256,1024]{1,0:T(8,128)(2,1)S(1)}, bf16[256,1024]{1,0:T(8,128)(2,1)S(1)}, u32[]{:S(2)}, u32[]{:S(2)}) collective-permute-start(bf16[256,1024]{1,0:T(8,128)(2,1)S(1)} %get-tuple-element.64.refs_1_), channel_id=1, source_target_pairs={{0,1},{1,2},{2,3},{3,0},{4,5},{5,6},{6,7},{7,4},{8,9},{9,10},{10,1... | collective-permute-start | bytes 1572872 | tf_op jit(solution)/shard_map/ppermute | solution.py:68
  14.9 27.7 %collective-permute-start.1 = (bf16[256,1024]{1,0:T(8,128)(2,1)S(1)}, bf16[256,1024]{1,0:T(8,128)(2,1)S(1)}, u32[]{:S(2)}, u32[]{:S(2)}) collective-permute-start(bf16[256,1024]{1,0:T(8,128)(2,1)S(1)} %get-tuple-element.59.refs_0_), channel_id=1, source_target_pairs={{0,3},{1,0},{2,1},{3,2},{4,7},{5,4},{6,5},{7,6},{8,11},{9,8},{10,9... | collective-permute-start | bytes 1572872 | tf_op jit(solution)/shard_map/ppermute | solution.py:68
  23.1 0.8 copy-start.8
  23.9 12.5 %copy-start.10 = (bf16[1408,128]{1,0:T(8,128)(2,1)}, bf16[1408,128]{1,0:T(8,128)(2,1)S(1)}, u32[]{:S(2)}) copy-start(bf16[1408,128]{1,0:T(8,128)(2,1)S(1)} %get-tuple-element.68.refs_2_.refs_4_) | copy-start | bytes 1081348
  23.9 12.5 %copy-start.12 = (bf16[1408,128]{1,0:T(8,128)(2,1)}, bf16[1408,128]{1,0:T(8,128)(2,1)S(1)}, u32[]{:S(2)}) copy-start(bf16[1408,128]{1,0:T(8,128)(2,1)S(1)} %get-tuple-element.69.refs_3_.refs_5_) | copy-start | bytes 1081348
  23.9 19.7 %collective-permute-start.9 = (bf16[512,512]{1,0:T(8,128)(2,1)S(1)}, bf16[512,512]{1,0:T(8,128)(2,1)S(1)}, u32[]{:S(2)}, u32[]{:S(2)}) collective-permute-start(bf16[512,512]{1,0:T(8,128)(2,1)S(1)} %get-tuple-element.71.refs_0_), channel_id=1, source_target_pairs={{0,8},{4,12},{8,0},{12,4},{16,24},{20,28},{24,16},{28,20},{32,40},... | collective-permute-start | bytes 1572872 | tf_op jit(solution)/shard_map/ppermute | solution.py:57
  29.6 16.1 %collective-permute-start.6 = (bf16[256,1024]{1,0:T(8,128)(2,1)S(1)}, bf16[256,1024]{1,0:T(8,128)(2,1)S(1)}, u32[]{:S(2)}, u32[]{:S(2)}) collective-permute-start(bf16[256,1024]{1,0:T(8,128)(2,1)S(1)} %collective-permute-done.2.refs_3_), channel_id=1, source_target_pairs={{0,3},{1,0},{2,1},{3,2},{4,7},{5,4},{6,5},{7,6},{8,11},{9,8},{10,9... | collective-permute-start | bytes 1572872 | tf_op jit(solution)/shard_map/ppermute | solution.py:68
  31.5 18.1 %collective-permute-start.5 = (bf16[256,1024]{1,0:T(8,128)(2,1)S(1)}, bf16[256,1024]{1,0:T(8,128)(2,1)S(1)}, u32[]{:S(2)}, u32[]{:S(2)}) collective-permute-start(bf16[256,1024]{1,0:T(8,128)(2,1)S(1)} %collective-permute-done.3.refs_6_), channel_id=1, source_target_pairs={{0,1},{1,2},{2,3},{3,0},{4,5},{5,6},{6,7},{7,4},{8,9},{9,10},{10,1... | collective-permute-start | bytes 1572872 | tf_op jit(solution)/shard_map/ppermute | solution.py:68
  36.4 0.8 copy-start.6
  38.4 21.2 %collective-permute-start.8 = (bf16[512,512]{1,0:T(8,128)(2,1)S(1)}, bf16[512,512]{1,0:T(8,128)(2,1)S(1)}, u32[]{:S(2)}, u32[]{:S(2)}) collective-permute-start(bf16[512,512]{1,0:T(8,128)(2,1)S(1)} %get-tuple-element.71.refs_0_), channel_id=1, source_target_pairs={{0,4},{4,0},{8,12},{12,8},{16,20},{20,16},{24,28},{28,24},{32,36},... | collective-permute-start | bytes 1572872 | tf_op jit(solution)/shard_map/ppermute | solution.py:57
  42.6 16.5 %collective-permute-start.12 = (bf16[512,512]{1,0:T(8,128)(2,1)S(1)}, bf16[512,512]{1,0:T(8,128)(2,1)S(1)}, u32[]{:S(2)}, u32[]{:S(2)}) collective-permute-start(bf16[512,512]{1,0:T(8,128)(2,1)S(1)} %get-tuple-element.74.refs_4_), channel_id=1, source_target_pairs={{0,8},{4,12},{8,0},{12,4},{16,24},{20,28},{24,16},{28,20},{32,40},... | collective-permute-start | bytes 1572872 | tf_op jit(solution)/shard_map/ppermute | solution.py:57
  43.6 19.4 %collective-permute-start.10 = (bf16[512,512]{1,0:T(8,128)(2,1)S(1)}, bf16[512,512]{1,0:T(8,128)(2,1)S(1)}, u32[]{:S(2)}, u32[]{:S(2)}) collective-permute-start(bf16[512,512]{1,0:T(8,128)(2,1)S(1)} %collective-permute-done.9.refs_2_), channel_id=1, source_target_pairs={{0,4},{4,0},{8,12},{12,8},{16,20},{20,16},{24,28},{28,24},{32,36},... | collective-permute-start | bytes 1572872 | tf_op jit(solution)/shard_map/ppermute | solution.py:57
  57.1 5.9 %collective-permute-start.11 = (bf16[512,512]{1,0:T(8,128)(2,1)S(1)}, bf16[512,512]{1,0:T(8,128)(2,1)S(1)}, u32[]{:S(2)}, u32[]{:S(2)}) collective-permute-start(bf16[512,512]{1,0:T(8,128)(2,1)S(1)} %get-tuple-element.74.refs_4_), channel_id=1, source_target_pairs={{0,4},{4,0},{8,12},{12,8},{16,20},{20,16},{24,28},{28,24},{32,36},... | collective-permute-start | bytes 1572872 | tf_op jit(solution)/shard_map/ppermute | solution.py:57
  59.1 3.9 %collective-permute-start.13 = (bf16[512,512]{1,0:T(8,128)(2,1)S(1)}, bf16[512,512]{1,0:T(8,128)(2,1)S(1)}, u32[]{:S(2)}, u32[]{:S(2)}) collective-permute-start(bf16[512,512]{1,0:T(8,128)(2,1)S(1)} %collective-permute-done.12.refs_6_), channel_id=1, source_target_pairs={{0,4},{4,0},{8,12},{12,8},{16,20},{20,16},{24,28},{28,24},{32,36},... | collective-permute-start | bytes 1572872 | tf_op jit(solution)/shard_map/ppermute | solution.py:57
  59.2 18.6 %collective-permute-start.14 = (bf16[512,512]{1,0:T(8,128)(2,1)S(1)}, bf16[512,512]{1,0:T(8,128)(2,1)S(1)}, u32[]{:S(2)}, u32[]{:S(2)}) collective-permute-start(bf16[512,512]{1,0:T(8,128)(2,1)S(1)} %get-tuple-element.95.refs_6_), channel_id=1, source_target_pairs={{0,4},{4,0},{8,12},{12,8},{16,20},{20,16},{24,28},{28,24},{32,36},... | collective-permute-start | bytes 1572872 | tf_op jit(solution)/shard_map/ppermute | solution.py:57
  59.6 21.4 %copy-start.9 = (bf16[4,128,512]{2,1,0:T(8,128)(2,1)S(1)}, bf16[4,128,512]{2,1,0:T(8,128)(2,1)}, u32[]{:S(2)}) copy-start(bf16[4,128,512]{2,1,0:T(8,128)(2,1)} %copy-done.8) | copy-start | bytes 1572868
  59.6 21.4 %copy-start.11 = (bf16[1408,128]{1,0:T(8,128)(2,1)S(1)}, bf16[1408,128]{1,0:T(8,128)(2,1)}, u32[]{:S(2)}) copy-start(bf16[1408,128]{1,0:T(8,128)(2,1)} %copy-done.10) | copy-start | bytes 1081348
  59.6 21.4 %copy-start.13 = (bf16[1408,128]{1,0:T(8,128)(2,1)S(1)}, bf16[1408,128]{1,0:T(8,128)(2,1)}, u32[]{:S(2)}) copy-start(bf16[1408,128]{1,0:T(8,128)(2,1)} %copy-done.12) | copy-start | bytes 1081348
  59.6 15.9 %collective-permute-start.16 = (bf16[512,512]{1,0:T(8,128)(2,1)S(1)}, bf16[512,512]{1,0:T(8,128)(2,1)S(1)}, u32[]{:S(2)}, u32[]{:S(2)}) collective-permute-start(bf16[512,512]{1,0:T(8,128)(2,1)S(1)} %get-tuple-element.81.refs_6_), channel_id=1, source_target_pairs={{0,8},{4,12},{8,0},{12,4},{16,24},{20,28},{24,16},{28,20},{32,40},... | collective-permute-start | bytes 1572872 | tf_op jit(solution)/shard_map/ppermute | solution.py:57
  63.0 0.8 copy-start.16
  75.4 5.5 %collective-permute-start.17 = (bf16[512,512]{1,0:T(8,128)(2,1)S(1)}, bf16[512,512]{1,0:T(8,128)(2,1)S(1)}, u32[]{:S(2)}, u32[]{:S(2)}) collective-permute-start(bf16[512,512]{1,0:T(8,128)(2,1)S(1)} %collective-permute-done.16.refs_8_), channel_id=1, source_target_pairs={{0,4},{4,0},{8,12},{12,8},{16,20},{20,16},{24,28},{28,24},{32,36},... | collective-permute-start | bytes 1572872 | tf_op jit(solution)/shard_map/ppermute | solution.py:57
  75.4 5.5 %collective-permute-start.15 = (bf16[512,512]{1,0:T(8,128)(2,1)S(1)}, bf16[512,512]{1,0:T(8,128)(2,1)S(1)}, u32[]{:S(2)}, u32[]{:S(2)}) collective-permute-start(bf16[512,512]{1,0:T(8,128)(2,1)S(1)} %get-tuple-element.81.refs_6_), channel_id=1, source_target_pairs={{0,4},{4,0},{8,12},{12,8},{16,20},{20,16},{24,28},{28,24},{32,36},... | collective-permute-start | bytes 1572872 | tf_op jit(solution)/shard_map/ppermute | solution.py:57
  76.0 13.9 %collective-permute-start.24 = (bf16[512,512]{1,0:T(8,128)(2,1)S(1)}, bf16[512,512]{1,0:T(8,128)(2,1)S(1)}, u32[]{:S(2)}, u32[]{:S(2)}) collective-permute-start(bf16[512,512]{1,0:T(8,128)(2,1)S(1)} %get-tuple-element.95.refs_6_), channel_id=1, source_target_pairs={{0,8},{4,12},{8,0},{12,4},{16,24},{20,28},{24,16},{28,20},{32,40},... | collective-permute-start | bytes 1572872 | tf_op jit(solution)/shard_map/ppermute | solution.py:57
  77.7 15.3 %collective-permute-start.18 = (bf16[512,512]{1,0:T(8,128)(2,1)S(1)}, bf16[512,512]{1,0:T(8,128)(2,1)S(1)}, u32[]{:S(2)}, u32[]{:S(2)}) collective-permute-start(bf16[512,512]{1,0:T(8,128)(2,1)S(1)} %get-tuple-element.86), channel_id=1, source_target_pairs={{0,1},{1,2},{2,3},{3,0},{4,5},{5,6},{6,7},{7,4},{8,9},{9,10},{10,1... | collective-permute-start | bytes 1572872 | tf_op jit(solution)/shard_map/ppermute | solution.py:68
  77.7 15.3 %collective-permute-start.19 = (bf16[512,512]{1,0:T(8,128)(2,1)S(1)}, bf16[512,512]{1,0:T(8,128)(2,1)S(1)}, u32[]{:S(2)}, u32[]{:S(2)}) collective-permute-start(bf16[512,512]{1,0:T(8,128)(2,1)S(1)} %get-tuple-element.87), channel_id=1, source_target_pairs={{0,3},{1,0},{2,1},{3,2},{4,7},{5,4},{6,5},{7,6},{8,11},{9,8},{10,9... | collective-permute-start | bytes 1572872 | tf_op jit(solution)/shard_map/ppermute | solution.py:68
  81.0 12.1 %copy-start.5 = (bf16[512,1024]{1,0:T(8,128)(2,1)S(1)}, bf16[512,1024]{1,0:T(8,128)(2,1)}, u32[]{:S(2)}) copy-start(bf16[512,1024]{1,0:T(8,128)(2,1)} %get-tuple-element.85.rows) | copy-start | bytes 3145732
  89.8 9.8 %collective-permute-start.25 = (bf16[512,512]{1,0:T(8,128)(2,1)S(1)}, bf16[512,512]{1,0:T(8,128)(2,1)S(1)}, u32[]{:S(2)}, u32[]{:S(2)}) collective-permute-start(bf16[512,512]{1,0:T(8,128)(2,1)S(1)} %collective-permute-done.24.refs_8_), channel_id=1, source_target_pairs={{0,4},{4,0},{8,12},{12,8},{16,20},{20,16},{24,28},{28,24},{32,36},... | collective-permute-start | bytes 1572872 | tf_op jit(solution)/shard_map/ppermute | solution.py:57
  89.8 17.0 %collective-permute-start.21 = (bf16[512,512]{1,0:T(8,128)(2,1)S(1)}, bf16[512,512]{1,0:T(8,128)(2,1)S(1)}, u32[]{:S(2)}, u32[]{:S(2)}) collective-permute-start(bf16[512,512]{1,0:T(8,128)(2,1)S(1)} %get-tuple-element.89), channel_id=1, source_target_pairs={{0,1},{1,2},{2,3},{3,0},{4,5},{5,6},{6,7},{7,4},{8,9},{9,10},{10,1... | collective-permute-start | bytes 1572872 | tf_op jit(solution)/shard_map/ppermute | solution.py:68
  89.8 17.0 %collective-permute-start.22 = (bf16[512,512]{1,0:T(8,128)(2,1)S(1)}, bf16[512,512]{1,0:T(8,128)(2,1)S(1)}, u32[]{:S(2)}, u32[]{:S(2)}) collective-permute-start(bf16[512,512]{1,0:T(8,128)(2,1)S(1)} %get-tuple-element.90), channel_id=1, source_target_pairs={{0,3},{1,0},{2,1},{3,2},{4,7},{5,4},{6,5},{7,6},{8,11},{9,8},{10,9... | collective-permute-start | bytes 1572872 | tf_op jit(solution)/shard_map/ppermute | solution.py:68
  93.1 6.6 %copy-start.7 = (bf16[4,128,512]{2,1,0:T(8,128)(2,1)S(1)}, bf16[4,128,512]{2,1,0:T(8,128)(2,1)}, u32[]{:S(2)}) copy-start(bf16[4,128,512]{2,1,0:T(8,128)(2,1)} %copy-done.6) | copy-start | bytes 1572868
  96.3 20.3 %collective-permute-start.20 = (bf16[512,512]{1,0:T(8,128)(2,1)S(1)}, bf16[512,512]{1,0:T(8,128)(2,1)S(1)}, u32[]{:S(2)}, u32[]{:S(2)}) collective-permute-start(bf16[512,512]{1,0:T(8,128)(2,1)S(1)} %get-tuple-element.88), channel_id=1, source_target_pairs={{0,1},{1,2},{2,3},{3,0},{4,5},{5,6},{6,7},{7,4},{8,9},{9,10},{10,1... | collective-permute-start | bytes 1572872 | tf_op jit(solution)/shard_map/ppermute | solution.py:68
  96.4 20.2 %collective-permute-start.23 = (bf16[512,512]{1,0:T(8,128)(2,1)S(1)}, bf16[512,512]{1,0:T(8,128)(2,1)S(1)}, u32[]{:S(2)}, u32[]{:S(2)}) collective-permute-start(bf16[512,512]{1,0:T(8,128)(2,1)S(1)} %get-tuple-element.91), channel_id=1, source_target_pairs={{0,3},{1,0},{2,1},{3,2},{4,7},{5,4},{6,5},{7,6},{8,11},{9,8},{10,9... | collective-permute-start | bytes 1572872 | tf_op jit(solution)/shard_map/ppermute | solution.py:68
  99.6 17.0 %copy-start.4 = (bf16[512,1024]{1,0:T(8,128)(2,1)S(1)}, bf16[512,1024]{1,0:T(8,128)(2,1)}, u32[]{:S(2)}) copy-start(bf16[512,1024]{1,0:T(8,128)(2,1)} %get-tuple-element.76.own) | copy-start | bytes 3145732
  106.8 14.6 %collective-permute-start.26 = (bf16[512,256]{1,0:T(8,128)(2,1)S(1)}, bf16[512,256]{1,0:T(8,128)(2,1)S(1)}, u32[]{:S(2)}, u32[]{:S(2)}) collective-permute-start(bf16[512,256]{1,0:T(8,128)(2,1)S(1)} %get-tuple-element.103), channel_id=1, source_target_pairs={{4,0},{8,4},{12,8},{16,12},{20,16},{24,20},{28,24},{32,28},{36,32}... | collective-permute-start | bytes 786440 | tf_op jit(solution)/shard_map/ppermute | solution.py:63
  108.7 12.7 %collective-permute-start.27 = (bf16[384,256]{1,0:T(8,128)(2,1)S(1)}, bf16[384,256]{1,0:T(8,128)(2,1)S(1)}, u32[]{:S(2)}, u32[]{:S(2)}) collective-permute-start(bf16[384,256]{1,0:T(8,128)(2,1)S(1)} %get-tuple-element.105), channel_id=1, source_target_pairs={{8,0},{12,4},{16,8},{20,12},{24,16},{28,20},{32,24},{36,28},{40,32... | collective-permute-start | bytes 589832 | tf_op jit(solution)/shard_map/ppermute | solution.py:63
where the time goes:
time: 124 us; the launch traced here: 122 us
  starting transfers between devices  46.8 us (38%)
  Pallas kernels  45.6 us (37%)
  waiting for transfers between devices  22.7 us (18%)
  local copies, waits for them, and re-layouts  5.53 us (4%)
    ppermute x12, starting transfers between devices, swap_cp(): return lax.ppermute(block, 'cp', [(i, i ^ mask) for i in range(count)])  19.2 us
    ppermute x12, starting transfers between devices, shift_tp(): lax.ppermute(block, 'tp', [(i, (i + distance) % count) for i in range(cou...  18 us
    pallas_call x2, Pallas kernels, backward(): pl.pallas_call(kernel, in_specs=[SMEM] + [WHOLE] * 5 + [ANY] * 4 + ([] if...  13.5 us
    ppermute x12, waiting for transfers between devices, shift_tp(): lax.ppermute(block, 'tp', [(i, (i + distance) % count) for i in range(cou...  13 us
    pallas_call x2, Pallas kernels, forward(): pl.pallas_call(kernel, in_specs=[SMEM, WHOLE] + ([ANY] * 3 if first else...  10.6 us
    ppermute x4, starting transfers between devices, shift_cp(): return lax.ppermute(block, 'cp', route)  9.59 us
    pallas_call x1, Pallas kernels, grad_matmul(): pl.pallas_call(grad_matmul_kernel, in_specs=[SMEM] + [WHOLE] * 8 + [ANY],...  7.48 us
    pallas_call x1, Pallas kernels, products(): pl.pallas_call(product_kernel, in_specs=[SMEM] + [ANY] * (4 * CHUNKS + 1)...  7.46 us
  transfers between devices with their start and end apart: 28, of which 7 were waited for; matrix products, arithmetic and copies ran while one was open for 0% of the time, Pallas kernels for 36%

commit v1 on v0

--- a/solution.py
+++ b/solution.py
@@ -610,8 +610,8 @@
 
     before_upper = shift_tp(upper, 1)
     ahead_lower = shift_tp(lower, -1)
-    before_lower = shift_tp(after(lower, far), 1)
-    ahead_upper = shift_tp(after(upper, far), -1)
+    before_lower = shift_tp(lower, 1)
+    ahead_upper = shift_tp(upper, -1)
 
     attended, attended_t, totals = [], [], []
     for chunk in range(CHUNKS):

time: 124 us -> 120 us (0.968)
  the two profiles are of different devices: /device:TPU:64 before, /device:TPU:24 now
where the time goes in v1:
time: 120 us; the launch traced here: 119 us
  Pallas kernels  52 us (43%)
  starting transfers between devices  34.4 us (29%)
  waiting for transfers between devices  26.3 us (22%)
  local copies, waits for them, and re-layouts  4.78 us (4%)
    ppermute x12, starting transfers between devices, shift_tp(): lax.ppermute(block, 'tp', [(i, (i + distance) % count) for i in range(cou...  18 us
    pallas_call x2, Pallas kernels, backward(): pl.pallas_call(kernel, in_specs=[SMEM] + [WHOLE] * 5 + [ANY] * 4 + ([] if...  16.3 us
    pallas_call x2, Pallas kernels, forward(): pl.pallas_call(kernel, in_specs=[SMEM, WHOLE] + ([ANY] * 3 if first else...  13.7 us
    ppermute x4, starting transfers between devices, shift_cp(): return lax.ppermute(block, 'cp', route)  12.3 us
    ppermute x4, waiting for transfers between devices, shift_cp(): return lax.ppermute(block, 'cp', route)  9.82 us
    ppermute x12, waiting for transfers between devices, swap_cp(): return lax.ppermute(block, 'cp', [(i, i ^ mask) for i in range(count)])  9.25 us
    pallas_call x1, Pallas kernels, grad_matmul(): pl.pallas_call(grad_matmul_kernel, in_specs=[SMEM] + [WHOLE] * 8 + [ANY],...  8.01 us
    pallas_call x1, Pallas kernels, products(): pl.pallas_call(product_kernel, in_specs=[SMEM] + [ANY] * (4 * CHUNKS + 1)...  7.39 us
  transfers between devices with their start and end apart: 28, of which 10 were waited for; matrix products, arithmetic and copies ran while one was open for 1% of the time, Pallas kernels for 42%

profile of v1, /device:TPU:24, one launch (start us, length us, event | category | flops | bytes accessed | tf_op | source)
XLA Modules:
  0.0 118.9 jit_solution(10788929154065548263)
XLA Ops:
  0.6 1.2 %copy-done = bf16[512,1024]{1,0:T(8,128)(2,1)S(1)} copy-done((bf16[512,1024]{1,0:T(8,128)(2,1)S(1)}, bf16[512,1024]{1,0:T(8,128)(2,1)}, u32[]{:S(2)}) %copy-start) | copy-done | bytes 1048600
  1.9 0.9 copy-done.2
  2.8 0.9 copy-done.3
  3.7 0.9 join.1
  4.6 1.6 %collective-permute-start.2 = (bf16[256,1024]{1,0:T(8,128)(2,1)S(1)}, bf16[256,1024]{1,0:T(8,128)(2,1)S(1)}, u32[]{:S(2)}, u32[]{:S(2)}) collective-permute-start(bf16[256,1024]{1,0:T(8,128)(2,1)S(1)} %get-tuple-element.54.refs_0_), channel_id=1, source_target_pairs={{0,1},{1,2},{2,3},{3,0},{4,5},{5,6},{6,7},{7,4},{8,9},{9,10},{10,1... | collective-permute-start | bytes 1572872 | tf_op jit(solution)/shard_map/ppermute | solution.py:68
  6.1 1.7 %collective-permute-start = (bf16[256,1024]{1,0:T(8,128)(2,1)S(1)}, bf16[256,1024]{1,0:T(8,128)(2,1)S(1)}, u32[]{:S(2)}, u32[]{:S(2)}) collective-permute-start(bf16[256,1024]{1,0:T(8,128)(2,1)S(1)} %get-tuple-element.54.refs_0_), channel_id=1, source_target_pairs={{0,3},{1,0},{2,1},{3,2},{4,7},{5,4},{6,5},{7,6},{8,11},{9,8},{10,9... | collective-permute-start | bytes 1572872 | tf_op jit(solution)/shard_map/ppermute | solution.py:68
  7.9 1.9 %collective-permute-start.4 = (bf16[512,256]{1,0:T(8,128)(2,1)S(1)}, bf16[512,256]{1,0:T(8,128)(2,1)}, u32[]{:S(2)}, u32[]{:S(2)}) collective-permute-start(bf16[512,256]{1,0:T(8,128)(2,1)S(1)} %get-tuple-element.56.refs_2_), channel_id=1, source_target_pairs={{0,4},{4,8},{8,12},{12,16},{16,20},{20,24},{24,28},{28,32},{32,36}... | collective-permute-start | bytes 786440 | tf_op jit(solution)/shard_map/ppermute | solution.py:63
  9.8 3.8 %collective-permute-start.3 = (bf16[384,256]{1,0:T(8,128)(2,1)}, bf16[384,256]{1,0:T(8,128)(2,1)}, u32[]{:S(2)}, u32[]{:S(2)}) collective-permute-start(bf16[384,256]{1,0:T(8,128)(2,1)} %get-tuple-element.57), channel_id=1, source_target_pairs={{0,8},{4,12},{8,16},{12,20},{16,24},{20,28},{24,32},{28,36},{32,40... | collective-permute-start | bytes 589832 | tf_op jit(solution)/shard_map/ppermute | solution.py:63
  13.6 1.6 %collective-permute-start.1 = (bf16[256,1024]{1,0:T(8,128)(2,1)S(1)}, bf16[256,1024]{1,0:T(8,128)(2,1)}, u32[]{:S(2)}, u32[]{:S(2)}) collective-permute-start(bf16[256,1024]{1,0:T(8,128)(2,1)S(1)} %get-tuple-element.55.refs_1_), channel_id=1, source_target_pairs={{0,3},{1,0},{2,1},{3,2},{4,7},{5,4},{6,5},{7,6},{8,11},{9,8},{10,9... | collective-permute-start | bytes 1572872 | tf_op jit(solution)/shard_map/ppermute | solution.py:68
  15.3 0.1 dynamic-slice_subtract_fusion
  15.3 0.1 select_reduce_fusion
  15.5 0.1 and_select_fusion
  15.5 0.1 and_select_fusion.2
  15.6 0.1 dynamic-slice_subtract_fusion.1
  15.7 0.1 fusion
  15.8 0.1 concatenate.3.refs_0_.table
  15.9 7.2 %collective-permute-done.3.refs_3_ = bf16[384,256]{1,0:T(8,128)(2,1)} collective-permute-done((bf16[384,256]{1,0:T(8,128)(2,1)}, bf16[384,256]{1,0:T(8,128)(2,1)}, u32[]{:S(2)}, u32[]{:S(2)}) %collective-permute-start.3) | collective-permute-done | bytes 196640 | tf_op jit(solution)/shard_map/ppermute | solution.py:63
  23.1 0.3 collective-permute-start.7
  23.3 0.0 collective-permute-done.4.refs_4_
  23.4 7.4 %attention_forward.2 = (bf16[512,512]{1,0:T(8,128)(2,1)S(1)}, bf16[4,128,512]{2,1,0:T(8,128)(2,1)S(1)}, f32[4,1,512]{2,1,0:T(1,128)S(1)}, bf16[1408,128]{1,0:T(8,128)(2,1)S(1)}, bf16[1408,128]{1,0:T(8,128)(2,1)S(1)}) custom-call(s32[22]{0:T(128)S(1)} %concatenate.3.refs_0_.table, bf16[512,1024]{1,0:T(8,128)(2,1)S(1)} %copy-done.1, ...), custom_call_target="tpu_custom_call" | custom-call | flops 9200000000 | bytes 28800000 | tf_op jit(solution)/shard_map/attention_forward/pallas_call | solution.py:186
  30.8 0.8 copy-done.8
  31.6 0.0 collective-permute-start.9
  31.6 0.0 collective-permute-done.1.refs_3_
  31.6 3.0 %collective-permute-start.6 = (bf16[256,1024]{1,0:T(8,128)(2,1)}, bf16[256,1024]{1,0:T(8,128)(2,1)S(1)}, u32[]{:S(2)}, u32[]{:S(2)}) collective-permute-start(bf16[256,1024]{1,0:T(8,128)(2,1)} %collective-permute-done.1.refs_3_), channel_id=1, source_target_pairs={{0,3},{1,0},{2,1},{3,2},{4,7},{5,4},{6,5},{7,6},{8,11},{9,8},{10,9... | collective-permute-start | bytes 1572872 | tf_op jit(solution)/shard_map/ppermute | solution.py:68
  34.7 6.3 %attention_forward.3 = (bf16[512,512]{1,0:T(8,128)(2,1)S(1)}, bf16[4,128,512]{2,1,0:T(8,128)(2,1)S(1)}, f32[4,1,512]{2,1,0:T(1,128)S(1)}) custom-call(s32[22]{0:T(128)S(1)} %concatenate.3.refs_0_.table, bf16[512,1024]{1,0:T(8,128)(2,1)S(1)} %copy-done.1, bf16[1408,128]{1,0:T(8,128)(2,1)S(1)} %get-tuple-element.64.refs_2_.refs_4_, ...), custom_call_target="tpu_custom_call" | custom-call | flops 9200000000 | bytes 28800000 | tf_op jit(solution)/shard_map/attention_forward/pallas_call | solution.py:186
  41.0 0.8 copy-done.6
  41.8 0.0 collective-permute-done.7.refs_7_
  41.8 0.0 collective-permute-start.12
  41.8 2.0 %collective-permute-start.8 = (bf16[512,512]{1,0:T(8,128)(2,1)S(1)}, bf16[512,512]{1,0:T(8,128)(2,1)S(1)}, u32[]{:S(2)}, u32[]{:S(2)}) collective-permute-start(bf16[512,512]{1,0:T(8,128)(2,1)S(1)} %get-tuple-element.67.refs_0_), channel_id=1, source_target_pairs={{0,4},{4,0},{8,12},{12,8},{16,20},{20,16},{24,28},{28,24},{32,36},... | collective-permute-start | bytes 1572872 | tf_op jit(solution)/shard_map/ppermute | solution.py:57
  43.8 0.4 collective-permute-done.9.refs_2_
  44.2 0.0 collective-permute-start.10
  44.2 2.3 %collective-permute-done.6.refs_5_ = bf16[256,1024]{1,0:T(8,128)(2,1)S(1)} collective-permute-done((bf16[256,1024]{1,0:T(8,128)(2,1)}, bf16[256,1024]{1,0:T(8,128)(2,1)S(1)}, u32[]{:S(2)}, u32[]{:S(2)}) %collective-permute-start.6) | collective-permute-done | bytes 524320 | tf_op jit(solution)/shard_map/ppermute | solution.py:68
  46.5 3.1 %collective-permute-done.5.refs_4_ = bf16[256,1024]{1,0:T(8,128)(2,1)S(1)} collective-permute-done((bf16[256,1024]{1,0:T(8,128)(2,1)S(1)}, bf16[256,1024]{1,0:T(8,128)(2,1)S(1)}, u32[]{:S(2)}, u32[]{:S(2)}) %collective-permute-start.5) | collective-permute-done | bytes 524320 | tf_op jit(solution)/shard_map/ppermute | solution.py:68
  49.6 8.0 %grad_projection.1 = (bf16[512,512]{1,0:T(8,128)(2,1)S(1)}, bf16[512,512]{1,0:T(8,128)(2,1)S(1)}) custom-call(s32[22]{0:T(128)S(1)} %concatenate.3.refs_0_.table, bf16[256,1024]{1,0:T(8,128)(2,1)S(1)} %get-tuple-element.54.refs_0_, bf16[256,1024]{1,0:T(8,128)(2,1)S(1)} %get-tuple-element.55.refs_1_, bf16[256,1024]{1,0:T(8,128)(2,1)S(1)} %collective-permute-done.refs_2_, ...), custom_call_target="tpu_custom_call" | custom-call | flops 8049999872 | bytes 25200000 | tf_op jit(solution)/shard_map/grad_projection/pallas_call | solution.py:380
  57.6 0.1 collective-permute-start.13
  57.7 0.5 collective-permute-start.11
  58.2 0.1 collective-permute-start.14
  58.3 0.0 collective-permute-done.8.refs_1_
  58.3 0.5 collective-permute-start.16
  58.8 0.0 collective-permute-done.10.refs_3_
  58.8 0.8 collective-permute-done.13.refs_7_
  59.6 0.7 collective-permute-done.11.refs_5_
  60.4 0.0 copy-done.16
  60.4 7.4 %products.1 = (bf16[512,512]{1,0:T(8,128)(2,1)S(1)}, bf16[512,512]{1,0:T(8,128)(2,1)S(1)}, bf16[512,512]{1,0:T(8,128)(2,1)S(1)}, bf16[512,512]{1,0:T(8,128)(2,1)...) custom-call(s32[22]{0:T(128)S(1)} %concatenate.3.refs_0_.table, ...), custom_call_target="tpu_custom_call" | custom-call | flops 8049999872 | bytes 25200000 | tf_op jit(solution)/shard_map/products/pallas_call | solution.py:436
  67.8 4.9 %collective-permute-done.16.refs_8_ = bf16[512,512]{1,0:T(8,128)(2,1)S(1)} collective-permute-done((bf16[512,512]{1,0:T(8,128)(2,1)S(1)}, bf16[512,512]{1,0:T(8,128)(2,1)S(1)}, u32[]{:S(2)}, u32[]{:S(2)}) %collective-permute-start.16) | collective-permute-done | bytes 524320 | tf_op jit(solution)/shard_map/ppermute | solution.py:57
  72.7 0.0 collective-permute-start.17
  72.7 0.5 collective-permute-start.15
  73.2 0.4 collective-permute-start.24
  73.6 0.6 collective-permute-start.18
  74.1 2.6 %collective-permute-start.19 = (bf16[512,512]{1,0:T(8,128)(2,1)S(1)}, bf16[512,512]{1,0:T(8,128)(2,1)S(1)}, u32[]{:S(2)}, u32[]{:S(2)}) collective-permute-start(bf16[512,512]{1,0:T(8,128)(2,1)S(1)} %get-tuple-element.83), channel_id=1, source_target_pairs={{0,3},{1,0},{2,1},{3,2},{4,7},{5,4},{6,5},{7,6},{8,11},{9,8},{10,9... | collective-permute-start | bytes 1572872 | tf_op jit(solution)/shard_map/ppermute | solution.py:68
  76.8 7.8 %attention_backward.2 = (bf16[512,1024]{1,0:T(8,128)(2,1)}, f32[1408,128]{1,0:T(8,128)S(1)}, f32[1408,128]{1,0:T(8,128)S(1)}) custom-call(s32[22]{0:T(128)S(1)} %concatenate.3.refs_0_.table, bf16[512,1024]{1,0:T(8,128)(2,1)S(1)} %copy-done.1, bf16[4,128,512]{2,1,0:T(8,128)(2,1)S(1)} %copy-done.9, f32[4,1,512]{2,1,0:T(1,128)S(1)} %get-tuple-element.75.refs_3_, ...), custom_call_target="tpu_custom_call" | custom-call | flops 10350000128 | bytes 32400000 | tf_op jit(solution)/shard_map/attention_backward/pallas_call | solution.py:332
  84.6 2.4 %collective-permute-done.24.refs_8_ = bf16[512,512]{1,0:T(8,128)(2,1)S(1)} collective-permute-done((bf16[512,512]{1,0:T(8,128)(2,1)S(1)}, bf16[512,512]{1,0:T(8,128)(2,1)S(1)}, u32[]{:S(2)}, u32[]{:S(2)}) %collective-permute-start.24) | collective-permute-done | bytes 524320 | tf_op jit(solution)/shard_map/ppermute | solution.py:57
  87.0 0.0 collective-permute-start.21
  87.0 3.2 %collective-permute-start.22 = (bf16[512,512]{1,0:T(8,128)(2,1)S(1)}, bf16[512,512]{1,0:T(8,128)(2,1)S(1)}, u32[]{:S(2)}, u32[]{:S(2)}) collective-permute-start(bf16[512,512]{1,0:T(8,128)(2,1)S(1)} %get-tuple-element.86), channel_id=1, source_target_pairs={{0,3},{1,0},{2,1},{3,2},{4,7},{5,4},{6,5},{7,6},{8,11},{9,8},{10,9... | collective-permute-start | bytes 1572872 | tf_op jit(solution)/shard_map/ppermute | solution.py:68
  90.3 3.2 %sum_products.1 = (bf16[512,512]{1,0:T(8,128)(2,1)S(1)}, bf16[512,512]{1,0:T(8,128)(2,1)S(1)}) custom-call(s32[22]{0:T(128)S(1)} %concatenate.3.refs_0_.table, bf16[512,1024]{1,0:T(8,128)(2,1)S(1)} %copy-done.5, bf16[1024,4096]{1,0:T(8,128)(2,1)} %weight_hbm.1, bf16[512,512]{1,0:T(8,128)(2,1)S(1)} %collective-permute-done.18.before, ...), custom_call_target="tpu_custom_call" | custom-call | flops 4600000000 | bytes 14400000 | tf_op jit(solution)/shard_map/sum_products/pallas_call | solution.py:468
  93.5 0.1 collective-permute-start.20
  93.6 3.2 %collective-permute-start.23 = (bf16[512,512]{1,0:T(8,128)(2,1)S(1)}, bf16[512,512]{1,0:T(8,128)(2,1)S(1)}, u32[]{:S(2)}, u32[]{:S(2)}) collective-permute-start(bf16[512,512]{1,0:T(8,128)(2,1)S(1)} %get-tuple-element.87), channel_id=1, source_target_pairs={{0,3},{1,0},{2,1},{3,2},{4,7},{5,4},{6,5},{7,6},{8,11},{9,8},{10,9... | collective-permute-start | bytes 1572872 | tf_op jit(solution)/shard_map/ppermute | solution.py:68
  96.8 8.6 %attention_backward.3 = (bf16[512,1024]{1,0:T(8,128)(2,1)}, f32[512,256]{1,0:T(8,128)S(1)}, bf16[512,256]{1,0:T(8,128)(2,1)S(1)}, bf16[384,256]{1,0:T(8,128)(2,1)S(1)}) custom-call(s32[22]{0:T(128)S(1)} %concatenate.3.refs_0_.table, bf16[512,1024]{1,0:T(8,128)(2,1)} %refs_1_.7, bf16[4,128,512]{2,1,0:T(8,128)(2,1)S(1)} %copy-done.7, ...), custom_call_target="tpu_custom_call", output_to_operand_aliasing={{0}: (10, {})} | custom-call | flops 10350000128 | bytes 32400000 | tf_op jit(solution)/shard_map/attention_backward/pallas_call | solution.py:332
  105.4 4.6 %collective-permute-start.26 = (bf16[512,256]{1,0:T(8,128)(2,1)S(1)}, bf16[512,256]{1,0:T(8,128)(2,1)S(1)}, u32[]{:S(2)}, u32[]{:S(2)}) collective-permute-start(bf16[512,256]{1,0:T(8,128)(2,1)S(1)} %get-tuple-element.99), channel_id=1, source_target_pairs={{4,0},{8,4},{12,8},{16,12},{20,16},{24,20},{28,24},{32,28},{36,32}... | collective-permute-start | bytes 786440 | tf_op jit(solution)/shard_map/ppermute | solution.py:63
  110.1 1.9 %collective-permute-start.27 = (bf16[384,256]{1,0:T(8,128)(2,1)S(1)}, bf16[384,256]{1,0:T(8,128)(2,1)S(1)}, u32[]{:S(2)}, u32[]{:S(2)}) collective-permute-start(bf16[384,256]{1,0:T(8,128)(2,1)S(1)} %get-tuple-element.101), channel_id=1, source_target_pairs={{8,0},{12,4},{16,8},{20,12},{24,16},{28,20},{32,24},{36,28},{40,32... | collective-permute-start | bytes 589832 | tf_op jit(solution)/shard_map/ppermute | solution.py:63
  112.0 1.8 %collective-permute-done.20.before_a = bf16[512,512]{1,0:T(8,128)(2,1)S(1)} collective-permute-done((bf16[512,512]{1,0:T(8,128)(2,1)S(1)}, bf16[512,512]{1,0:T(8,128)(2,1)S(1)}, u32[]{:S(2)}, u32[]{:S(2)}) %collective-permute-start.20) | collective-permute-done | bytes 524320 | tf_op jit(solution)/shard_map/ppermute | solution.py:68
  113.8 1.7 %last_sum.1 = bf16[512,1024]{1,0:T(8,128)(2,1)} custom-call(bf16[512,1024]{1,0:T(8,128)(2,1)S(1)} %copy-done.4, bf16[512,512]{1,0:T(8,128)(2,1)S(1)} %collective-permute-done.20.before_a, bf16[512,512]{1,0:T(8,128)(2,1)S(1)} %collective-permute-done.21.before_b, bf16[512,512]{1,0:T(8,128)(2,1)S(1)} %collective-permute-done.22.after_a, ...), custom_call_target="tpu_custom_call" | custom-call | flops 2300000000 | bytes 7200000 | tf_op jit(solution)/shard_map/last_sum/pallas_call | solution.py:494
  115.5 2.6 %collective-permute-done.27.far = bf16[384,256]{1,0:T(8,128)(2,1)S(1)} collective-permute-done((bf16[384,256]{1,0:T(8,128)(2,1)S(1)}, bf16[384,256]{1,0:T(8,128)(2,1)S(1)}, u32[]{:S(2)}, u32[]{:S(2)}) %collective-permute-start.27) | collective-permute-done | bytes 196640 | tf_op jit(solution)/shard_map/ppermute | solution.py:63
  118.1 0.8 add_terms.1
  (43 shorter events, 0.1 us)
Async XLA Ops:
  0.6 1.2 %copy-start = (bf16[512,1024]{1,0:T(8,128)(2,1)S(1)}, bf16[512,1024]{1,0:T(8,128)(2,1)}, u32[]{:S(2)}) copy-start(bf16[512,1024]{1,0:T(8,128)(2,1)} %grads.1) | copy-start | bytes 3145732
  1.9 0.9 copy-start.2
  2.8 0.9 copy-start.3
  3.7 11.6 %copy-start.14 = (s32[256]{0:T(256)S(1)}, s32[256]{0:T(256)}, u32[]{:S(2)}) copy-start(s32[256]{0:T(256)} %param.13) | copy-start | bytes 3076
  3.7 12.0 %copy-start.15 = (s32[256]{0:T(256)S(1)}, s32[256]{0:T(256)}, u32[]{:S(2)}) copy-start(s32[256]{0:T(256)} %param.12) | copy-start | bytes 3076
  3.7 19.7 %copy-start.1 = (bf16[512,1024]{1,0:T(8,128)(2,1)S(1)}, bf16[512,1024]{1,0:T(8,128)(2,1)}, u32[]{:S(2)}) copy-start(bf16[512,1024]{1,0:T(8,128)(2,1)} %refs_1_.7) | copy-start | bytes 3145732
  4.6 27.0 %collective-permute-start.2 = (bf16[256,1024]{1,0:T(8,128)(2,1)S(1)}, bf16[256,1024]{1,0:T(8,128)(2,1)S(1)}, u32[]{:S(2)}, u32[]{:S(2)}) collective-permute-start(bf16[256,1024]{1,0:T(8,128)(2,1)S(1)} %get-tuple-element.54.refs_0_), channel_id=1, source_target_pairs={{0,1},{1,2},{2,3},{3,0},{4,5},{5,6},{6,7},{7,4},{8,9},{9,10},{10,1... | collective-permute-start | bytes 1572872 | tf_op jit(solution)/shard_map/ppermute | solution.py:68
  6.1 35.6 %collective-permute-start = (bf16[256,1024]{1,0:T(8,128)(2,1)S(1)}, bf16[256,1024]{1,0:T(8,128)(2,1)S(1)}, u32[]{:S(2)}, u32[]{:S(2)}) collective-permute-start(bf16[256,1024]{1,0:T(8,128)(2,1)S(1)} %get-tuple-element.54.refs_0_), channel_id=1, source_target_pairs={{0,3},{1,0},{2,1},{3,2},{4,7},{5,4},{6,5},{7,6},{8,11},{9,8},{10,9... | collective-permute-start | bytes 1572872 | tf_op jit(solution)/shard_map/ppermute | solution.py:68
  7.9 15.5 %collective-permute-start.4 = (bf16[512,256]{1,0:T(8,128)(2,1)S(1)}, bf16[512,256]{1,0:T(8,128)(2,1)}, u32[]{:S(2)}, u32[]{:S(2)}) collective-permute-start(bf16[512,256]{1,0:T(8,128)(2,1)S(1)} %get-tuple-element.56.refs_2_), channel_id=1, source_target_pairs={{0,4},{4,8},{8,12},{12,16},{16,20},{20,24},{24,28},{28,32},{32,36}... | collective-permute-start | bytes 786440 | tf_op jit(solution)/shard_map/ppermute | solution.py:63
  9.8 13.3 %collective-permute-start.3 = (bf16[384,256]{1,0:T(8,128)(2,1)}, bf16[384,256]{1,0:T(8,128)(2,1)}, u32[]{:S(2)}, u32[]{:S(2)}) collective-permute-start(bf16[384,256]{1,0:T(8,128)(2,1)} %get-tuple-element.57), channel_id=1, source_target_pairs={{0,8},{4,12},{8,16},{12,20},{16,24},{20,28},{24,32},{28,36},{32,40... | collective-permute-start | bytes 589832 | tf_op jit(solution)/shard_map/ppermute | solution.py:63
  13.6 18.0 %collective-permute-start.1 = (bf16[256,1024]{1,0:T(8,128)(2,1)S(1)}, bf16[256,1024]{1,0:T(8,128)(2,1)}, u32[]{:S(2)}, u32[]{:S(2)}) collective-permute-start(bf16[256,1024]{1,0:T(8,128)(2,1)S(1)} %get-tuple-element.55.refs_1_), channel_id=1, source_target_pairs={{0,3},{1,0},{2,1},{3,2},{4,7},{5,4},{6,5},{7,6},{8,11},{9,8},{10,9... | collective-permute-start | bytes 1572872 | tf_op jit(solution)/shard_map/ppermute | solution.py:68
  23.1 18.7 %collective-permute-start.7 = (bf16[256,1024]{1,0:T(8,128)(2,1)S(1)}, bf16[256,1024]{1,0:T(8,128)(2,1)S(1)}, u32[]{:S(2)}, u32[]{:S(2)}) collective-permute-start(bf16[256,1024]{1,0:T(8,128)(2,1)S(1)} %get-tuple-element.55.refs_1_), channel_id=1, source_target_pairs={{0,1},{1,2},{2,3},{3,0},{4,5},{5,6},{6,7},{7,4},{8,9},{9,10},{10,1... | collective-permute-start | bytes 1572872 | tf_op jit(solution)/shard_map/ppermute | solution.py:68
  30.8 0.8 copy-start.8
  31.6 9.3 %copy-start.10 = (bf16[1408,128]{1,0:T(8,128)(2,1)}, bf16[1408,128]{1,0:T(8,128)(2,1)S(1)}, u32[]{:S(2)}) copy-start(bf16[1408,128]{1,0:T(8,128)(2,1)S(1)} %get-tuple-element.64.refs_2_.refs_4_) | copy-start | bytes 1081348
  31.6 9.3 %copy-start.12 = (bf16[1408,128]{1,0:T(8,128)(2,1)}, bf16[1408,128]{1,0:T(8,128)(2,1)S(1)}, u32[]{:S(2)}) copy-start(bf16[1408,128]{1,0:T(8,128)(2,1)S(1)} %get-tuple-element.65.refs_3_.refs_5_) | copy-start | bytes 1081348
  31.6 12.6 %collective-permute-start.9 = (bf16[512,512]{1,0:T(8,128)(2,1)S(1)}, bf16[512,512]{1,0:T(8,128)(2,1)S(1)}, u32[]{:S(2)}, u32[]{:S(2)}) collective-permute-start(bf16[512,512]{1,0:T(8,128)(2,1)S(1)} %get-tuple-element.67.refs_0_), channel_id=1, source_target_pairs={{0,8},{4,12},{8,0},{12,4},{16,24},{20,28},{24,16},{28,20},{32,40},... | collective-permute-start | bytes 1572872 | tf_op jit(solution)/shard_map/ppermute | solution.py:57
  31.6 14.9 %collective-permute-start.6 = (bf16[256,1024]{1,0:T(8,128)(2,1)}, bf16[256,1024]{1,0:T(8,128)(2,1)S(1)}, u32[]{:S(2)}, u32[]{:S(2)}) collective-permute-start(bf16[256,1024]{1,0:T(8,128)(2,1)} %collective-permute-done.1.refs_3_), channel_id=1, source_target_pairs={{0,3},{1,0},{2,1},{3,2},{4,7},{5,4},{6,5},{7,6},{8,11},{9,8},{10,9... | collective-permute-start | bytes 1572872 | tf_op jit(solution)/shard_map/ppermute | solution.py:68
  34.6 14.9 %collective-permute-start.5 = (bf16[256,1024]{1,0:T(8,128)(2,1)S(1)}, bf16[256,1024]{1,0:T(8,128)(2,1)S(1)}, u32[]{:S(2)}, u32[]{:S(2)}) collective-permute-start(bf16[256,1024]{1,0:T(8,128)(2,1)S(1)} %collective-permute-done.2.refs_6_), channel_id=1, source_target_pairs={{0,1},{1,2},{2,3},{3,0},{4,5},{5,6},{6,7},{7,4},{8,9},{9,10},{10,1... | collective-permute-start | bytes 1572872 | tf_op jit(solution)/shard_map/ppermute | solution.py:68
  41.0 0.8 copy-start.6
  41.8 15.8 %collective-permute-start.12 = (bf16[512,512]{1,0:T(8,128)(2,1)S(1)}, bf16[512,512]{1,0:T(8,128)(2,1)S(1)}, u32[]{:S(2)}, u32[]{:S(2)}) collective-permute-start(bf16[512,512]{1,0:T(8,128)(2,1)S(1)} %get-tuple-element.70.refs_4_), channel_id=1, source_target_pairs={{0,8},{4,12},{8,0},{12,4},{16,24},{20,28},{24,16},{28,20},{32,40},... | collective-permute-start | bytes 1572872 | tf_op jit(solution)/shard_map/ppermute | solution.py:57
  41.8 16.5 %collective-permute-start.8 = (bf16[512,512]{1,0:T(8,128)(2,1)S(1)}, bf16[512,512]{1,0:T(8,128)(2,1)S(1)}, u32[]{:S(2)}, u32[]{:S(2)}) collective-permute-start(bf16[512,512]{1,0:T(8,128)(2,1)S(1)} %get-tuple-element.67.refs_0_), channel_id=1, source_target_pairs={{0,4},{4,0},{8,12},{12,8},{16,20},{20,16},{24,28},{28,24},{32,36},... | collective-permute-start | bytes 1572872 | tf_op jit(solution)/shard_map/ppermute | solution.py:57
  44.2 14.6 %collective-permute-start.10 = (bf16[512,512]{1,0:T(8,128)(2,1)S(1)}, bf16[512,512]{1,0:T(8,128)(2,1)S(1)}, u32[]{:S(2)}, u32[]{:S(2)}) collective-permute-start(bf16[512,512]{1,0:T(8,128)(2,1)S(1)} %collective-permute-done.9.refs_2_), channel_id=1, source_target_pairs={{0,4},{4,0},{8,12},{12,8},{16,20},{20,16},{24,28},{28,24},{32,36},... | collective-permute-start | bytes 1572872 | tf_op jit(solution)/shard_map/ppermute | solution.py:57
  57.6 2.0 %collective-permute-start.13 = (bf16[512,512]{1,0:T(8,128)(2,1)S(1)}, bf16[512,512]{1,0:T(8,128)(2,1)S(1)}, u32[]{:S(2)}, u32[]{:S(2)}) collective-permute-start(bf16[512,512]{1,0:T(8,128)(2,1)S(1)} %collective-permute-done.12.refs_6_), channel_id=1, source_target_pairs={{0,4},{4,0},{8,12},{12,8},{16,20},{20,16},{24,28},{28,24},{32,36},... | collective-permute-start | bytes 1572872 | tf_op jit(solution)/shard_map/ppermute | solution.py:57
  57.7 2.6 %collective-permute-start.11 = (bf16[512,512]{1,0:T(8,128)(2,1)S(1)}, bf16[512,512]{1,0:T(8,128)(2,1)S(1)}, u32[]{:S(2)}, u32[]{:S(2)}) collective-permute-start(bf16[512,512]{1,0:T(8,128)(2,1)S(1)} %get-tuple-element.70.refs_4_), channel_id=1, source_target_pairs={{0,4},{4,0},{8,12},{12,8},{16,20},{20,16},{24,28},{28,24},{32,36},... | collective-permute-start | bytes 1572872 | tf_op jit(solution)/shard_map/ppermute | solution.py:57
  58.2 15.0 %collective-permute-start.14 = (bf16[512,512]{1,0:T(8,128)(2,1)S(1)}, bf16[512,512]{1,0:T(8,128)(2,1)S(1)}, u32[]{:S(2)}, u32[]{:S(2)}) collective-permute-start(bf16[512,512]{1,0:T(8,128)(2,1)S(1)} %get-tuple-element.91.refs_6_), channel_id=1, source_target_pairs={{0,4},{4,0},{8,12},{12,8},{16,20},{20,16},{24,28},{28,24},{32,36},... | collective-permute-start | bytes 1572872 | tf_op jit(solution)/shard_map/ppermute | solution.py:57
  58.3 18.5 %copy-start.9 = (bf16[4,128,512]{2,1,0:T(8,128)(2,1)S(1)}, bf16[4,128,512]{2,1,0:T(8,128)(2,1)}, u32[]{:S(2)}) copy-start(bf16[4,128,512]{2,1,0:T(8,128)(2,1)} %copy-done.8) | copy-start | bytes 1572868
  58.3 18.5 %copy-start.11 = (bf16[1408,128]{1,0:T(8,128)(2,1)S(1)}, bf16[1408,128]{1,0:T(8,128)(2,1)}, u32[]{:S(2)}) copy-start(bf16[1408,128]{1,0:T(8,128)(2,1)} %copy-done.10) | copy-start | bytes 1081348
  58.3 18.5 %copy-start.13 = (bf16[1408,128]{1,0:T(8,128)(2,1)S(1)}, bf16[1408,128]{1,0:T(8,128)(2,1)}, u32[]{:S(2)}) copy-start(bf16[1408,128]{1,0:T(8,128)(2,1)} %copy-done.12) | copy-start | bytes 1081348
  58.3 14.3 %collective-permute-start.16 = (bf16[512,512]{1,0:T(8,128)(2,1)S(1)}, bf16[512,512]{1,0:T(8,128)(2,1)S(1)}, u32[]{:S(2)}, u32[]{:S(2)}) collective-permute-start(bf16[512,512]{1,0:T(8,128)(2,1)S(1)} %get-tuple-element.77.refs_6_), channel_id=1, source_target_pairs={{0,8},{4,12},{8,0},{12,4},{16,24},{20,28},{24,16},{28,20},{32,40},... | collective-permute-start | bytes 1572872 | tf_op jit(solution)/shard_map/ppermute | solution.py:57
  59.6 0.8 copy-start.16
  72.7 4.1 %collective-permute-start.17 = (bf16[512,512]{1,0:T(8,128)(2,1)S(1)}, bf16[512,512]{1,0:T(8,128)(2,1)S(1)}, u32[]{:S(2)}, u32[]{:S(2)}) collective-permute-start(bf16[512,512]{1,0:T(8,128)(2,1)S(1)} %collective-permute-done.16.refs_8_), channel_id=1, source_target_pairs={{0,4},{4,0},{8,12},{12,8},{16,20},{20,16},{24,28},{28,24},{32,36},... | collective-permute-start | bytes 1572872 | tf_op jit(solution)/shard_map/ppermute | solution.py:57
  72.7 4.1 %collective-permute-start.15 = (bf16[512,512]{1,0:T(8,128)(2,1)S(1)}, bf16[512,512]{1,0:T(8,128)(2,1)S(1)}, u32[]{:S(2)}, u32[]{:S(2)}) collective-permute-start(bf16[512,512]{1,0:T(8,128)(2,1)S(1)} %get-tuple-element.77.refs_6_), channel_id=1, source_target_pairs={{0,4},{4,0},{8,12},{12,8},{16,20},{20,16},{24,28},{28,24},{32,36},... | collective-permute-start | bytes 1572872 | tf_op jit(solution)/shard_map/ppermute | solution.py:57
  73.2 13.8 %collective-permute-start.24 = (bf16[512,512]{1,0:T(8,128)(2,1)S(1)}, bf16[512,512]{1,0:T(8,128)(2,1)S(1)}, u32[]{:S(2)}, u32[]{:S(2)}) collective-permute-start(bf16[512,512]{1,0:T(8,128)(2,1)S(1)} %get-tuple-element.91.refs_6_), channel_id=1, source_target_pairs={{0,8},{4,12},{8,0},{12,4},{16,24},{20,28},{24,16},{28,20},{32,40},... | collective-permute-start | bytes 1572872 | tf_op jit(solution)/shard_map/ppermute | solution.py:57
  73.6 16.7 %collective-permute-start.18 = (bf16[512,512]{1,0:T(8,128)(2,1)S(1)}, bf16[512,512]{1,0:T(8,128)(2,1)S(1)}, u32[]{:S(2)}, u32[]{:S(2)}) collective-permute-start(bf16[512,512]{1,0:T(8,128)(2,1)S(1)} %get-tuple-element.82), channel_id=1, source_target_pairs={{0,1},{1,2},{2,3},{3,0},{4,5},{5,6},{6,7},{7,4},{8,9},{9,10},{10,1... | collective-permute-start | bytes 1572872 | tf_op jit(solution)/shard_map/ppermute | solution.py:68
  74.1 16.1 %collective-permute-start.19 = (bf16[512,512]{1,0:T(8,128)(2,1)S(1)}, bf16[512,512]{1,0:T(8,128)(2,1)S(1)}, u32[]{:S(2)}, u32[]{:S(2)}) collective-permute-start(bf16[512,512]{1,0:T(8,128)(2,1)S(1)} %get-tuple-element.83), channel_id=1, source_target_pairs={{0,3},{1,0},{2,1},{3,2},{4,7},{5,4},{6,5},{7,6},{8,11},{9,8},{10,9... | collective-permute-start | bytes 1572872 | tf_op jit(solution)/shard_map/ppermute | solution.py:68
  76.8 13.4 %copy-start.5 = (bf16[512,1024]{1,0:T(8,128)(2,1)S(1)}, bf16[512,1024]{1,0:T(8,128)(2,1)}, u32[]{:S(2)}) copy-start(bf16[512,1024]{1,0:T(8,128)(2,1)} %get-tuple-element.81.rows) | copy-start | bytes 3145732
  87.0 9.8 %collective-permute-start.25 = (bf16[512,512]{1,0:T(8,128)(2,1)S(1)}, bf16[512,512]{1,0:T(8,128)(2,1)S(1)}, u32[]{:S(2)}, u32[]{:S(2)}) collective-permute-start(bf16[512,512]{1,0:T(8,128)(2,1)S(1)} %collective-permute-done.24.refs_8_), channel_id=1, source_target_pairs={{0,4},{4,0},{8,12},{12,8},{16,20},{20,16},{24,28},{28,24},{32,36},... | collective-permute-start | bytes 1572872 | tf_op jit(solution)/shard_map/ppermute | solution.py:57
  87.0 18.4 %collective-permute-start.21 = (bf16[512,512]{1,0:T(8,128)(2,1)S(1)}, bf16[512,512]{1,0:T(8,128)(2,1)S(1)}, u32[]{:S(2)}, u32[]{:S(2)}) collective-permute-start(bf16[512,512]{1,0:T(8,128)(2,1)S(1)} %get-tuple-element.85), channel_id=1, source_target_pairs={{0,1},{1,2},{2,3},{3,0},{4,5},{5,6},{6,7},{7,4},{8,9},{9,10},{10,1... | collective-permute-start | bytes 1572872 | tf_op jit(solution)/shard_map/ppermute | solution.py:68
  87.0 18.4 %collective-permute-start.22 = (bf16[512,512]{1,0:T(8,128)(2,1)S(1)}, bf16[512,512]{1,0:T(8,128)(2,1)S(1)}, u32[]{:S(2)}, u32[]{:S(2)}) collective-permute-start(bf16[512,512]{1,0:T(8,128)(2,1)S(1)} %get-tuple-element.86), channel_id=1, source_target_pairs={{0,3},{1,0},{2,1},{3,2},{4,7},{5,4},{6,5},{7,6},{8,11},{9,8},{10,9... | collective-permute-start | bytes 1572872 | tf_op jit(solution)/shard_map/ppermute | solution.py:68
  90.3 6.6 %copy-start.7 = (bf16[4,128,512]{2,1,0:T(8,128)(2,1)S(1)}, bf16[4,128,512]{2,1,0:T(8,128)(2,1)}, u32[]{:S(2)}) copy-start(bf16[4,128,512]{2,1,0:T(8,128)(2,1)} %copy-done.6) | copy-start | bytes 1572868
  93.5 20.3 %collective-permute-start.20 = (bf16[512,512]{1,0:T(8,128)(2,1)S(1)}, bf16[512,512]{1,0:T(8,128)(2,1)S(1)}, u32[]{:S(2)}, u32[]{:S(2)}) collective-permute-start(bf16[512,512]{1,0:T(8,128)(2,1)S(1)} %get-tuple-element.84), channel_id=1, source_target_pairs={{0,1},{1,2},{2,3},{3,0},{4,5},{5,6},{6,7},{7,4},{8,9},{9,10},{10,1... | collective-permute-start | bytes 1572872 | tf_op jit(solution)/shard_map/ppermute | solution.py:68
  93.6 20.2 %collective-permute-start.23 = (bf16[512,512]{1,0:T(8,128)(2,1)S(1)}, bf16[512,512]{1,0:T(8,128)(2,1)S(1)}, u32[]{:S(2)}, u32[]{:S(2)}) collective-permute-start(bf16[512,512]{1,0:T(8,128)(2,1)S(1)} %get-tuple-element.87), channel_id=1, source_target_pairs={{0,3},{1,0},{2,1},{3,2},{4,7},{5,4},{6,5},{7,6},{8,11},{9,8},{10,9... | collective-permute-start | bytes 1572872 | tf_op jit(solution)/shard_map/ppermute | solution.py:68
  96.8 17.0 %copy-start.4 = (bf16[512,1024]{1,0:T(8,128)(2,1)S(1)}, bf16[512,1024]{1,0:T(8,128)(2,1)}, u32[]{:S(2)}) copy-start(bf16[512,1024]{1,0:T(8,128)(2,1)} %get-tuple-element.72.own) | copy-start | bytes 3145732
  105.4 12.7 %collective-permute-start.26 = (bf16[512,256]{1,0:T(8,128)(2,1)S(1)}, bf16[512,256]{1,0:T(8,128)(2,1)S(1)}, u32[]{:S(2)}, u32[]{:S(2)}) collective-permute-start(bf16[512,256]{1,0:T(8,128)(2,1)S(1)} %get-tuple-element.99), channel_id=1, source_target_pairs={{4,0},{8,4},{12,8},{16,12},{20,16},{24,20},{28,24},{32,28},{36,32}... | collective-permute-start | bytes 786440 | tf_op jit(solution)/shard_map/ppermute | solution.py:63
  110.1 8.1 %collective-permute-start.27 = (bf16[384,256]{1,0:T(8,128)(2,1)S(1)}, bf16[384,256]{1,0:T(8,128)(2,1)S(1)}, u32[]{:S(2)}, u32[]{:S(2)}) collective-permute-start(bf16[384,256]{1,0:T(8,128)(2,1)S(1)} %get-tuple-element.101), channel_id=1, source_target_pairs={{8,0},{12,4},{16,8},{20,12},{24,16},{28,20},{32,24},{36,28},{40,32... | collective-permute-start | bytes 589832 | tf_op jit(solution)/shard_map/ppermute | solution.py:63
